TPU v7x, 256 devices: a whole 4x4x8 slice. The times are simulated.
256 devices in a mesh: blk: 64 (over y, x, z_hi), rows: 4 (over z_lo, core).
Axes of the slice: x: 4, y: 4, z: 8 (z_hi: 4, z_lo: 2; z = z_hi * 2 + z_lo), core: 2. Of those that a mesh axis runs over, the one named last changes fastest.
Arguments:
- sens_tiles: bfloat16 [16384, 512, 128], P('blk', 'rows'), may hold values from -1 to 1
- start_basis: bfloat16 [64, 262144], P(None, 'blk'), may hold values from -6 to 6
- row_blocks: int32 [16384, 4], P('blk', 'rows'), may hold values from 0 to 7, as said below
- col_blocks: int32 [16384, 4], P('blk', 'rows'), may hold values from 0 to 31, as said below
- live_counts: int32 [64, 4], P('blk', 'rows'), may hold values from 64 to 256, as said below
Outputs:
- orthonormal: float32 [4, 64, 262144], P(None, None, ('blk', 'rows'))
Inputs may be any that keep to these rules, and one draw needn't show every extreme that they name: Within one device the pairs (row_blocks, col_blocks) of its 256 slots are distinct. Within one device the pairs (row_blocks, col_blocks) of its 256 slots are distinct. Slots 0 to live_counts - 1 of a device hold its tiles; some device has all 256 slots live.
All inputs are finite; a program needn't handle non-finite values.
Results may differ from a plain program's by a relative error of at most 0.012.
The roundings to bfloat16 on the way count: a program that leaves them out, or rounds other values in their place, can miss the bound.
Values may be sent and summed in bfloat16 or wider, within the bound.
No kernel may reach another device: no remote copies, remote signals or barrier semaphores. Data moves between devices by JAX's collectives and lax.ppermute only.
A program may use at most 128 MiB of HBM per device.

v0:
```python
import jax
import jax.numpy as jnp
from jax import lax
from jax.experimental import pallas as pl
from jax.experimental.pallas import tpu as pltpu
from jax.sharding import Mesh
from jax.sharding import PartitionSpec as P

TILE = 128
K = 64
RB = 8
CB = 32
MAXB = 256
ITERS = 4
CELLS = 262144.0
WIDTH = CB * TILE
HEIGHT = RB * TILE
HALF = WIDTH // 2
OWN = WIDTH // 4
PEERS = 16
EACH = 5
PANEL = 4
BATCHES = 8
BATCH = MAXB // BATCHES

f32 = jnp.float32
bf16 = jnp.bfloat16
BLK = ("y", "x", "h")
ROWS = ("l", "c")
PLANE = ("y", "x")
VMEM = pl.BlockSpec(memory_space=pltpu.VMEM)
SMEM = pl.BlockSpec(memory_space=pltpu.SMEM)
HBM = pl.BlockSpec(memory_space=pltpu.HBM)


def dot_rows(a, b):
    return lax.dot_general(a, b, (((1,), (1,)), ((), ())), preferred_element_type=f32)


def params(mib):
    return pltpu.CompilerParams(vmem_limit_bytes=mib << 20)


def write_packed(out, image, gram):
    for n in range(PEERS * EACH):
        rows = pl.ds((n % EACH) * 8, 8)
        if n < 64:
            g, j = divmod(n, 8)
            out[n // EACH, rows, :] = image[g * 8 : g * 8 + 8, j * TILE : (j + 1) * TILE]
        elif n < 72 and gram is not None:
            g = n - 64
            out[n // EACH, rows, :] = gram[g * 8 : g * 8 + 8, :]
        else:
            out[n // EACH, rows, :] = jnp.zeros((8, TILE), f32)


def read_packed(packed, n):
    return packed[n // EACH, pl.ds((n % EACH) * 8, 8), :]


def two_parts(x):
    high = x.astype(bf16)
    low = (x - high.astype(f32)).astype(bf16)
    return jnp.concatenate([high, low], axis=0)


def gram_of(parts):
    four = dot_rows(parts, parts)
    two = four[:K] + four[K:]
    return two[:, :K] + two[:, K:]


def reciprocal(x):
    near = pl.reciprocal(x, approx=True)
    near = near * (2.0 - x * near)
    return near * (2.0 - x * near)


def inverse_factor(gram):
    shape = (K, 2 * K)
    row = lax.broadcasted_iota(jnp.int32, shape, 0)
    col = lax.broadcasted_iota(jnp.int32, shape, 1)
    work = jnp.concatenate([gram, (row[:, :K] == col[:, :K]).astype(f32)], axis=1)
    for k in range(0, K, PANEL):
        columns = [jnp.broadcast_to(work[:, k + j : k + j + 1], shape) for j in range(PANEL)]
        lines = [work[k + j : k + j + 1, :] for j in range(PANEL)]
        for j in range(PANEL):
            at = k + j
            inverse = reciprocal(columns[j][at : at + 1, :])
            factor = jnp.where(row > at, columns[j] * inverse, 0.0)
            for later in range(j + 1, PANEL):
                columns[later] = columns[later] - factor * columns[later][at : at + 1, :]
                to = k + later
                lines[later] = lines[later] - factor[to : to + 1, :] * lines[j]
            work = work - factor * lines[j]
    diagonal = jnp.sum(jnp.where(row == col, work, 0.0), axis=1, keepdims=True)
    return work[:, K:] * lax.rsqrt(diagonal)


def load(dense, held, sems):
    copies = []
    for p in range(4):
        span = pl.ds(p * OWN, OWN)
        copies.append(pltpu.make_async_copy(dense.at[:, span], held.at[:, span], sems.at[p]))
        copies[-1].start()
    return copies


def start_kernel(row_blocks, col_blocks, live, turn, tiles, basis, dense, packed, stock, first, held, sems, first_sem, out_sem):
    get_basis = pltpu.make_async_copy(basis, first, first_sem)
    get_basis.start()
    copies = []
    for n in range(BATCHES):
        span = pl.ds(n * BATCH, BATCH)
        copies.append(pltpu.make_async_copy(tiles.at[span], stock.at[span], sems.at[n]))
        copies[-1].start()
    core, count = turn[0], live[0]

    def window(s):
        col = col_blocks[s]
        quarter = col // (CB // 4)
        position = (((quarter % 2) ^ core) * 2 + quarter // 2) * (CB // 4) + col % (CB // 4)
        return (
            pl.ds(pl.multiple_of(row_blocks[s] * TILE, TILE), TILE),
            pl.ds(pl.multiple_of(position * TILE, TILE), TILE),
        )

    def put(s, carry):
        held[window(s)] = stock[s]
        return carry

    def clear(s, carry):
        held[window(s)] = jnp.zeros((TILE, TILE), bf16)
        return carry

    for n in range(BATCHES):
        copies[n].wait()
        middle = jnp.clip(count, n * BATCH, (n + 1) * BATCH)
        lax.fori_loop(n * BATCH, middle, put, 0)
        lax.fori_loop(middle, (n + 1) * BATCH, clear, 0)
    away = pltpu.make_async_copy(held, dense, out_sem)
    away.start()
    get_basis.wait()
    image = jnp.zeros((K, HEIGHT), f32)
    for p in range(4):
        q = (p % 2) * 2 + ((p // 2) ^ core)
        part = first[:, pl.ds(pl.multiple_of(q * OWN, OWN), OWN)]
        image = image + dot_rows(part, held[:, p * OWN : (p + 1) * OWN])
    write_packed(packed, image, None)
    away.wait()


def forward_kernel(mine, other, dense, packed, held, sems):
    copies = load(dense, held, sems)
    image = jnp.zeros((2 * K, HEIGHT), f32)
    grams = []
    for p, half in enumerate((mine, other)):
        parts = two_parts(half[...])
        grams.append(gram_of(parts))
        for n in range(2):
            q = p * 2 + n
            copies[q].wait()
            image = image + dot_rows(parts[:, n * OWN : (n + 1) * OWN], held[:, q * OWN : (q + 1) * OWN])
    gram = grams[0] + grams[1]
    write_packed(packed, image[:K] + image[K:], jnp.concatenate([gram, gram], axis=1))


def gram_kernel(own, out):
    gram = gram_of(two_parts(own[...]))
    out[...] = jnp.concatenate([gram[: K // 2], gram[K // 2 :]], axis=1)


def image_of(packed):
    return jnp.concatenate(
        [jnp.concatenate([read_packed(packed, g * 8 + j) for j in range(8)], axis=1) for g in range(8)],
        axis=0,
    )


def spread(image_half, copies, held, mine, other):
    for p in range(4):
        copies[p].wait()
        target = mine if p < 2 else other
        for n in range(2):
            source = pl.ds(p * OWN + n * OWN // 2, OWN // 2)
            product = jnp.dot(image_half, held[:, source], preferred_element_type=f32)
            target[:, pl.ds((p % 2) * OWN + n * OWN // 2, OWN // 2)] = product


def first_backward_kernel(packed, dense, mine, other, held, sems):
    copies = load(dense, held, sems)
    spread(image_of(packed).astype(bf16), copies, held, mine, other)


def backward_kernel(packed, dense, mine, other, inverse, held, sems):
    copies = load(dense, held, sems)
    gram = jnp.concatenate([read_packed(packed, 64 + g) for g in range(8)], axis=0)[:, :K]
    found = inverse_factor(gram * (1.0 / CELLS))
    inverse[...] = found
    image = jnp.dot(found, image_of(packed), precision=lax.Precision.HIGHEST, preferred_element_type=f32)
    spread(image.astype(bf16), copies, held, mine, other)


def finish_kernel(turn, gram, *refs):
    halves, inverses, out = refs[:ITERS], refs[ITERS:-1], refs[-1]
    own = pl.ds(pl.multiple_of(turn[1] * OWN, OWN), OWN)
    whole = jnp.concatenate([gram[:, :K], gram[:, K:]], axis=0)
    last = inverse_factor(whole * (1.0 / CELLS))
    for i in range(ITERS):
        found, taken = (inverses[i][...], halves[i][:, own]) if i < ITERS - 1 else (last, halves[i][...])
        out[i] = jnp.dot(found, taken, precision=lax.Precision.HIGHEST, preferred_element_type=f32)


def shifted(x, axis, by):
    count = lax.axis_size(axis)
    return lax.ppermute(x, axis, [(i, (i + by) % count) for i in range(count)])


def summed_by_all(x, axes):
    count = lax.axis_size(axes)
    return jnp.sum(lax.all_to_all(jnp.broadcast_to(x[None], (count, *x.shape)), axes, 0, 0, tiled=True), axis=0)


def summed_over_blk(packed):
    shares = lax.all_to_all(packed, PLANE, 0, 0, tiled=True)
    total = summed_by_all(jnp.sum(shares, axis=0), "h")
    return lax.all_to_all(jnp.broadcast_to(total[None], packed.shape), PLANE, 0, 0, tiled=True)


def local(sens_tiles, start_basis, row_blocks, col_blocks, live_counts):
    core, low = lax.axis_index("c"), lax.axis_index("l")
    turn = jnp.stack([core, low]).astype(jnp.int32)
    packed_shape = jax.ShapeDtypeStruct((PEERS, EACH * 8, TILE), f32)
    half_shape = jax.ShapeDtypeStruct((K, HALF), f32)
    square_shape = jax.ShapeDtypeStruct((K, K), f32)
    dense_shape = jax.ShapeDtypeStruct((HEIGHT, WIDTH), bf16)
    holding = [pltpu.VMEM((HEIGHT, WIDTH), bf16), pltpu.SemaphoreType.DMA((4,))]
    dense, packed = pl.pallas_call(
        start_kernel,
        out_shape=(dense_shape, packed_shape),
        in_specs=[SMEM, SMEM, SMEM, SMEM, HBM, HBM],
        out_specs=(HBM, VMEM),
        scratch_shapes=[
            pltpu.VMEM(sens_tiles.shape, bf16),
            pltpu.VMEM(start_basis.shape, bf16),
            pltpu.VMEM((HEIGHT, WIDTH), bf16),
            pltpu.SemaphoreType.DMA((BATCHES,)),
            pltpu.SemaphoreType.DMA,
            pltpu.SemaphoreType.DMA,
        ],
        compiler_params=params(57),
    )(row_blocks.reshape(MAXB), col_blocks.reshape(MAXB), live_counts.reshape(1), turn, sens_tiles, start_basis)
    halves, inverses = [], []
    for iteration in range(ITERS):
        packed = summed_over_blk(packed)
        first = iteration == 0
        mine, other, *inverse = pl.pallas_call(
            first_backward_kernel if first else backward_kernel,
            out_shape=(half_shape, half_shape) if first else (half_shape, half_shape, square_shape),
            in_specs=[VMEM, HBM],
            out_specs=(VMEM, VMEM) if first else (VMEM, VMEM, VMEM),
            scratch_shapes=holding,
            compiler_params=params(50),
        )(packed, dense)
        inverses += inverse
        mine = mine + shifted(other, "c", 1)
        if iteration == ITERS - 1:
            kept = lax.dynamic_slice_in_dim(mine, low * OWN, OWN, 1)
            sent = lax.dynamic_slice_in_dim(mine, (1 - low) * OWN, OWN, 1)
            halves.append(kept + shifted(sent, "l", 1))
            break
        mine = mine + shifted(mine, "l", 1)
        halves.append(mine)
        packed = pl.pallas_call(
            forward_kernel,
            out_shape=packed_shape,
            in_specs=[VMEM, VMEM, HBM],
            out_specs=VMEM,
            scratch_shapes=holding,
            compiler_params=params(50),
        )(mine, shifted(mine, "c", 1), dense)
    gram = pl.pallas_call(
        gram_kernel,
        out_shape=jax.ShapeDtypeStruct((K // 2, 2 * K), f32),
        in_specs=[VMEM],
        out_specs=VMEM,
        compiler_params=params(50),
    )(halves[-1])
    gram = summed_by_all(summed_by_all(gram, PLANE + ("c",)), ("h", "l"))
    return pl.pallas_call(
        finish_kernel,
        out_shape=jax.ShapeDtypeStruct((ITERS, K, OWN), f32),
        in_specs=[SMEM] + [VMEM] * (2 * ITERS),
        out_specs=VMEM,
        compiler_params=params(50),
    )(turn, gram, *halves, *inverses)


def solution(mesh):
    fine = Mesh(mesh.devices.reshape(4, 4, 4, 2, 2), BLK + ROWS)
    in_specs = (
        P(BLK, ROWS, None),
        P(None, BLK),
        P(BLK, ROWS),
        P(BLK, ROWS),
        P(BLK, ROWS),
    )
    out_specs = P(None, None, BLK + ROWS)
    return jax.shard_map(local, mesh=fine, in_specs=in_specs, out_specs=out_specs, check_vma=False)
```

profile of v0, /device:TPU:2, one launch (start us, length us, event | category | flops | bytes accessed | tf_op | source)
XLA Modules:
  0.0 303.6 jit_solution(9871802847656199482)
XLA Ops:
  1.3 12.3 %shard_map.55 = (bf16[1024,4096]{1,0:T(8,128)(2,1)}, f32[16,40,128]{2,1,0:T(8,128)}) custom-call(s32[256]{0:T(256)} %bitcast.6, s32[256]{0:T(256)} %bitcast.7, s32[1]{0:T(128)} %bitcast.5.live, s32[2]{0:T(128)} %pad_add_fusion.turn, bf16[256,128,128]{2,1,0:T(8,128)(2,1)} %tiles.1, bf16[64,4096]{1,0:T(8,128)(2,1)} %basis.1), custom_call_target="tpu_custom_call" | custom-call | tf_op jit(solution)/shard_map/pallas_call | solution.py:238
  13.6 15.5 %all_to_all.70 = f32[16,40,128]{2,1,0:T(8,128)S(1)} all-to-all(f32[16,40,128]{2,1,0:T(8,128)} %get-tuple-element.18), channel_id=1, replica_groups=mesh['y'=4,'x'=4,'h'=4,'l'=2,'c'=2] {'y','x'}, dimensions={0} | all-to-all | bytes 655360 | tf_op jit(solution)/shard_map/all_to_all | solution.py:225
  29.1 16.6 %all_to_all.71 = f32[4,40,128]{2,1,0:T(8,128)S(1)} all-to-all(f32[4,40,128]{2,1,0:T(8,128)S(1)} %broadcast_in_dim.20), channel_id=1, replica_groups=mesh['y'=4,'x'=4,'h'=4,'l'=2,'c'=2] {'h'}, dimensions={0} | all-to-all | bytes 163840 | tf_op jit(solution)/shard_map/all_to_all | solution.py:221
  45.8 11.9 %all_to_all.72.packed = f32[16,40,128]{2,1,0:T(8,128)S(1)} all-to-all(f32[16,40,128]{2,1,0:T(8,128)S(1)} %broadcast_in_dim.21), channel_id=1, replica_groups=mesh['y'=4,'x'=4,'h'=4,'l'=2,'c'=2] {'y','x'}, dimensions={0} | all-to-all | bytes 655360 | tf_op jit(solution)/shard_map/all_to_all | solution.py:227
  64.9 12.9 %collective-permute-done.1 = f32[64,2048]{1,0:T(8,128)S(1)} collective-permute-done((f32[64,2048]{1,0:T(8,128)S(1)}, f32[64,2048]{1,0:T(8,128)S(1)}, u32[]{:S(2)}, u32[]{:S(2)}) %collective-permute-start.1) | collective-permute-done | bytes 524320 | tf_op jit(solution)/shard_map/ppermute | solution.py:216
  85.3 12.6 %all_to_all.73 = f32[16,40,128]{2,1,0:T(8,128)S(1)} all-to-all(f32[16,40,128]{2,1,0:T(8,128)S(1)} %shard_map.57), channel_id=1, replica_groups=mesh['y'=4,'x'=4,'h'=4,'l'=2,'c'=2] {'y','x'}, dimensions={0} | all-to-all | bytes 655360 | tf_op jit(solution)/shard_map/all_to_all | solution.py:225
  97.9 10.7 %all_to_all.74 = f32[4,40,128]{2,1,0:T(8,128)S(1)} all-to-all(f32[4,40,128]{2,1,0:T(8,128)S(1)} %broadcast_in_dim.22), channel_id=1, replica_groups=mesh['y'=4,'x'=4,'h'=4,'l'=2,'c'=2] {'h'}, dimensions={0} | all-to-all | bytes 163840 | tf_op jit(solution)/shard_map/all_to_all | solution.py:221
  108.7 11.9 %all_to_all.75.packed = f32[16,40,128]{2,1,0:T(8,128)S(1)} all-to-all(f32[16,40,128]{2,1,0:T(8,128)S(1)} %broadcast_in_dim.23), channel_id=1, replica_groups=mesh['y'=4,'x'=4,'h'=4,'l'=2,'c'=2] {'y','x'}, dimensions={0} | all-to-all | bytes 655360 | tf_op jit(solution)/shard_map/all_to_all | solution.py:227
  120.5 7.3 %shard_map.58 = (f32[64,2048]{1,0:T(8,128)S(1)}, f32[64,2048]{1,0:T(8,128)S(1)}, f32[64,64]{1,0:T(8,128)S(1)}) custom-call(f32[16,40,128]{2,1,0:T(8,128)S(1)} %all_to_all.75.packed, bf16[1024,4096]{1,0:T(8,128)(2,1)} %get-tuple-element.19.dense), custom_call_target="tpu_custom_call" | custom-call | tf_op jit(solution)/shard_map/pallas_call | solution.py:257
  130.8 13.1 %collective-permute-done.4 = f32[64,2048]{1,0:T(8,128)S(1)} collective-permute-done((f32[64,2048]{1,0:T(8,128)S(1)}, f32[64,2048]{1,0:T(8,128)S(1)}, u32[]{:S(2)}, u32[]{:S(2)}) %collective-permute-start.4) | collective-permute-done | bytes 524320 | tf_op jit(solution)/shard_map/ppermute | solution.py:216
  146.2 5.4 %shard_map.59 = f32[16,40,128]{2,1,0:T(8,128)S(1)} custom-call(f32[64,2048]{1,0:T(8,128)S(1)} %add.33.mine.refs_1_, f32[64,2048]{1,0:T(8,128)S(1)} %collective-permute-done.5.other, bf16[1024,4096]{1,0:T(8,128)(2,1)} %get-tuple-element.19.dense), custom_call_target="tpu_custom_call" | custom-call | tf_op jit(solution)/shard_map/pallas_call | solution.py:274
  151.6 12.6 %all_to_all.76 = f32[16,40,128]{2,1,0:T(8,128)S(1)} all-to-all(f32[16,40,128]{2,1,0:T(8,128)S(1)} %shard_map.59), channel_id=1, replica_groups=mesh['y'=4,'x'=4,'h'=4,'l'=2,'c'=2] {'y','x'}, dimensions={0} | all-to-all | bytes 655360 | tf_op jit(solution)/shard_map/all_to_all | solution.py:225
  164.2 10.7 %all_to_all.77 = f32[4,40,128]{2,1,0:T(8,128)S(1)} all-to-all(f32[4,40,128]{2,1,0:T(8,128)S(1)} %broadcast_in_dim.24), channel_id=1, replica_groups=mesh['y'=4,'x'=4,'h'=4,'l'=2,'c'=2] {'h'}, dimensions={0} | all-to-all | bytes 163840 | tf_op jit(solution)/shard_map/all_to_all | solution.py:221
  174.9 11.9 %all_to_all.78.packed = f32[16,40,128]{2,1,0:T(8,128)S(1)} all-to-all(f32[16,40,128]{2,1,0:T(8,128)S(1)} %broadcast_in_dim.25), channel_id=1, replica_groups=mesh['y'=4,'x'=4,'h'=4,'l'=2,'c'=2] {'y','x'}, dimensions={0} | all-to-all | bytes 655360 | tf_op jit(solution)/shard_map/all_to_all | solution.py:227
  186.8 7.3 %shard_map.60 = (f32[64,2048]{1,0:T(8,128)S(1)}, f32[64,2048]{1,0:T(8,128)S(1)}, f32[64,64]{1,0:T(8,128)S(1)}) custom-call(f32[16,40,128]{2,1,0:T(8,128)S(1)} %all_to_all.78.packed, bf16[1024,4096]{1,0:T(8,128)(2,1)} %get-tuple-element.19.dense), custom_call_target="tpu_custom_call" | custom-call | tf_op jit(solution)/shard_map/pallas_call | solution.py:257
  197.2 13.0 %collective-permute-done.7 = f32[64,2048]{1,0:T(8,128)S(1)} collective-permute-done((f32[64,2048]{1,0:T(8,128)S(1)}, f32[64,2048]{1,0:T(8,128)S(1)}, u32[]{:S(2)}, u32[]{:S(2)}) %collective-permute-start.7) | collective-permute-done | bytes 524320 | tf_op jit(solution)/shard_map/ppermute | solution.py:216
  212.3 5.4 %shard_map.61 = f32[16,40,128]{2,1,0:T(8,128)S(1)} custom-call(f32[64,2048]{1,0:T(8,128)S(1)} %add.35.mine.refs_2_, f32[64,2048]{1,0:T(8,128)S(1)} %collective-permute-done.8.other, bf16[1024,4096]{1,0:T(8,128)(2,1)} %get-tuple-element.19.dense), custom_call_target="tpu_custom_call" | custom-call | tf_op jit(solution)/shard_map/pallas_call | solution.py:274
  217.7 12.6 %all_to_all.79 = f32[16,40,128]{2,1,0:T(8,128)S(1)} all-to-all(f32[16,40,128]{2,1,0:T(8,128)S(1)} %shard_map.61), channel_id=1, replica_groups=mesh['y'=4,'x'=4,'h'=4,'l'=2,'c'=2] {'y','x'}, dimensions={0} | all-to-all | bytes 655360 | tf_op jit(solution)/shard_map/all_to_all | solution.py:225
  230.3 10.7 %all_to_all.80 = f32[4,40,128]{2,1,0:T(8,128)S(1)} all-to-all(f32[4,40,128]{2,1,0:T(8,128)S(1)} %broadcast_in_dim.26), channel_id=1, replica_groups=mesh['y'=4,'x'=4,'h'=4,'l'=2,'c'=2] {'h'}, dimensions={0} | all-to-all | bytes 163840 | tf_op jit(solution)/shard_map/all_to_all | solution.py:221
  241.1 11.9 %all_to_all.81.packed = f32[16,40,128]{2,1,0:T(8,128)S(1)} all-to-all(f32[16,40,128]{2,1,0:T(8,128)S(1)} %broadcast_in_dim.27), channel_id=1, replica_groups=mesh['y'=4,'x'=4,'h'=4,'l'=2,'c'=2] {'y','x'}, dimensions={0} | all-to-all | bytes 655360 | tf_op jit(solution)/shard_map/all_to_all | solution.py:227
  253.0 7.3 %shard_map.62 = (f32[64,2048]{1,0:T(8,128)S(1)}, f32[64,2048]{1,0:T(8,128)S(1)}, f32[64,64]{1,0:T(8,128)S(1)}) custom-call(f32[16,40,128]{2,1,0:T(8,128)S(1)} %all_to_all.81.packed, bf16[1024,4096]{1,0:T(8,128)(2,1)} %get-tuple-element.19.dense), custom_call_target="tpu_custom_call" | custom-call | tf_op jit(solution)/shard_map/pallas_call | solution.py:257
  263.2 7.6 %collective-permute-done.10 = f32[64,1024]{1,0:T(8,128)S(1)} collective-permute-done((f32[64,1024]{1,0:T(8,128)S(1)}, f32[64,1024]{1,0:T(8,128)S(1)}, u32[]{:S(2)}, u32[]{:S(2)}) %collective-permute-start.10) | collective-permute-done | bytes 262176 | tf_op jit(solution)/shard_map/ppermute | solution.py:216
  271.3 14.9 %all_to_all.82 = f32[32,32,128]{2,1,0:T(8,128)S(1)} all-to-all(f32[32,32,128]{2,1,0:T(8,128)S(1)} %broadcast_in_dim.28), channel_id=1, replica_groups=mesh['y'=4,'x'=4,'h'=4,'l'=2,'c'=2] {'y','x','c'}, dimensions={0} | all-to-all | bytes 1048576 | tf_op jit(solution)/shard_map/all_to_all | solution.py:221
  286.2 12.3 %all_to_all.83 = f32[8,32,128]{2,1,0:T(8,128)S(1)} all-to-all(f32[8,32,128]{2,1,0:T(8,128)S(1)} %broadcast_in_dim.29), channel_id=1, replica_groups=mesh['y'=4,'x'=4,'h'=4,'l'=2,'c'=2] {'h','l'}, dimensions={0} | all-to-all | bytes 262144 | tf_op jit(solution)/shard_map/all_to_all | solution.py:221
  (54 shorter events, 34.3 us)
Async XLA Ops:
  61.7 2.0 collective-permute-start
  63.8 14.1 %collective-permute-start.1 = (f32[64,2048]{1,0:T(8,128)S(1)}, f32[64,2048]{1,0:T(8,128)S(1)}, u32[]{:S(2)}, u32[]{:S(2)}) collective-permute-start(f32[64,2048]{1,0:T(8,128)S(1)} %add.30), channel_id=1, source_target_pairs={{0,2},{2,0},{1,3},{3,1},{4,6},{6,4},{5,7},{7,5},{8,10},{10,8},{9,1... | collective-permute-start | bytes 1572872 | tf_op jit(solution)/shard_map/ppermute | solution.py:216
  77.9 2.0 collective-permute-start.2
  127.8 2.0 collective-permute-start.3
  129.9 14.1 %collective-permute-start.4 = (f32[64,2048]{1,0:T(8,128)S(1)}, f32[64,2048]{1,0:T(8,128)S(1)}, u32[]{:S(2)}, u32[]{:S(2)}) collective-permute-start(f32[64,2048]{1,0:T(8,128)S(1)} %add.32), channel_id=1, source_target_pairs={{0,2},{2,0},{1,3},{3,1},{4,6},{6,4},{5,7},{7,5},{8,10},{10,8},{9,1... | collective-permute-start | bytes 1572872 | tf_op jit(solution)/shard_map/ppermute | solution.py:216
  144.0 2.2 collective-permute-start.5
  194.1 2.0 collective-permute-start.6
  196.2 14.1 %collective-permute-start.7 = (f32[64,2048]{1,0:T(8,128)S(1)}, f32[64,2048]{1,0:T(8,128)S(1)}, u32[]{:S(2)}, u32[]{:S(2)}) collective-permute-start(f32[64,2048]{1,0:T(8,128)S(1)} %add.34), channel_id=1, source_target_pairs={{0,2},{2,0},{1,3},{3,1},{4,6},{6,4},{5,7},{7,5},{8,10},{10,8},{9,1... | collective-permute-start | bytes 1572872 | tf_op jit(solution)/shard_map/ppermute | solution.py:216
  210.3 2.0 collective-permute-start.8
  217.7 80.8 %copy-start = (s32[2]{0:T(128)S(1)}, s32[2]{0:T(128)}, u32[]{:S(2)}) copy-start(s32[2]{0:T(128)} %pad_add_fusion.turn) | copy-start | bytes 28
  260.3 2.0 collective-permute-start.9
  262.4 8.4 %collective-permute-start.10 = (f32[64,1024]{1,0:T(8,128)S(1)}, f32[64,1024]{1,0:T(8,128)S(1)}, u32[]{:S(2)}, u32[]{:S(2)}) collective-permute-start(f32[64,1024]{1,0:T(8,128)S(1)} %constant_dynamic-slice_fusion), channel_id=1, source_target_pairs={{0,2},{2,0},{1,3},{3,1},{4,6},{6,4},{5,7},{7,5},{8,10},{10,8},{9,1... | collective-permute-start | bytes 786440 | tf_op jit(solution)/shard_map/ppermute | solution.py:216
where the time goes:
time: 305 us; the launch traced here: 304 us
  blocking collectives  177 us (58%)
  waiting for transfers between devices  60 us (20%)
  Pallas kernels  59.8 us (20%)
  starting transfers between devices  4.66 us (2%)
    all_to_all x6, blocking collectives, summed_by_all(): lax.all_to_all(jnp.broadcast_to(x[None], (count, *x.shape)), axes, 0, 0,...  75.8 us
    ppermute x11, waiting for transfers between devices, shifted(): return lax.ppermute(x, axis, [(i, (i + by) % count) for i in range(count)])  60 us
    all_to_all x4, blocking collectives, summed_over_blk(): shares = lax.all_to_all(packed, PLANE, 0, 0, tiled=True)  53.2 us
    all_to_all x4, blocking collectives, summed_over_blk(): lax.all_to_all(jnp.broadcast_to(total[None], packed.shape), PLANE, 0, 0,...  47.6 us
    pallas_call x4, Pallas kernels, local(): pl.pallas_call(first_backward_kernel if first else backward_kernel, out_s...  25.8 us
    pallas_call x3, Pallas kernels, local(): pl.pallas_call(forward_kernel, out_shape=packed_shape, in_specs=[VMEM, VM...  16.2 us
    pallas_call x1, Pallas kernels, local(): pl.pallas_call(start_kernel, out_shape=(dense_shape, packed_shape), in_sp...  12.3 us
  transfers between devices with their start and end apart: 11, of which 11 were waited for; matrix products, arithmetic and copies ran while one was open for 0% of the time, Pallas kernels for 0%

commit v1 on v0

v1 whole, which is shorter than its diff:
```python
import jax
import jax.numpy as jnp
from jax import lax
from jax.experimental import pallas as pl
from jax.experimental.pallas import tpu as pltpu
from jax.sharding import Mesh
from jax.sharding import PartitionSpec as P

TILE = 128
K = 64
RB = 8
CB = 32
MAXB = 256
ITERS = 4
CELLS = 262144.0
WIDTH = CB * TILE
HEIGHT = RB * TILE
HALF = WIDTH // 2
OWN = WIDTH // 4
PEERS = 16
EACH = 5
PANEL = 4
START_MIB = 40
BATCHES = 8
BATCH = MAXB // BATCHES

f32 = jnp.float32
bf16 = jnp.bfloat16
BLK = ("y", "x", "h")
ROWS = ("l", "c")
PLANE = ("y", "x")
VMEM = pl.BlockSpec(memory_space=pltpu.VMEM)
SMEM = pl.BlockSpec(memory_space=pltpu.SMEM)
HBM = pl.BlockSpec(memory_space=pltpu.HBM)


def dot_rows(a, b):
    return lax.dot_general(a, b, (((1,), (1,)), ((), ())), preferred_element_type=f32)


def params(mib):
    return pltpu.CompilerParams(vmem_limit_bytes=mib << 20)


def write_packed(out, image, gram):
    for n in range(PEERS * EACH):
        rows = pl.ds((n % EACH) * 8, 8)
        if n < 64:
            g, j = divmod(n, 8)
            out[n // EACH, rows, :] = image[g * 8 : g * 8 + 8, j * TILE : (j + 1) * TILE]
        elif n < 72 and gram is not None:
            g = n - 64
            out[n // EACH, rows, :] = gram[g * 8 : g * 8 + 8, :]
        else:
            out[n // EACH, rows, :] = jnp.zeros((8, TILE), f32)


def read_packed(packed, n):
    return packed[n // EACH, pl.ds((n % EACH) * 8, 8), :]


def two_parts(x):
    high = x.astype(bf16)
    low = (x - high.astype(f32)).astype(bf16)
    return jnp.concatenate([high, low], axis=0)


def gram_of(parts):
    four = dot_rows(parts, parts)
    two = four[:K] + four[K:]
    return two[:, :K] + two[:, K:]


def reciprocal(x):
    near = pl.reciprocal(x, approx=True)
    near = near * (2.0 - x * near)
    return near * (2.0 - x * near)


def inverse_factor(gram):
    shape = (K, 2 * K)
    row = lax.broadcasted_iota(jnp.int32, shape, 0)
    col = lax.broadcasted_iota(jnp.int32, shape, 1)
    work = jnp.concatenate([gram, (row[:, :K] == col[:, :K]).astype(f32)], axis=1)
    for k in range(0, K, PANEL):
        columns = [jnp.broadcast_to(work[:, k + j : k + j + 1], shape) for j in range(PANEL)]
        lines = [work[k + j : k + j + 1, :] for j in range(PANEL)]
        for j in range(PANEL):
            at = k + j
            inverse = reciprocal(columns[j][at : at + 1, :])
            factor = jnp.where(row > at, columns[j] * inverse, 0.0)
            for later in range(j + 1, PANEL):
                columns[later] = columns[later] - factor * columns[later][at : at + 1, :]
                to = k + later
                lines[later] = lines[later] - factor[to : to + 1, :] * lines[j]
            work = work - factor * lines[j]
    diagonal = jnp.sum(jnp.where(row == col, work, 0.0), axis=1, keepdims=True)
    return work[:, K:] * lax.rsqrt(diagonal)


def start_kernel(row_blocks, col_blocks, live, turn, tiles, basis, dense, packed, stock, first, sems, first_sem):
    get_basis = pltpu.make_async_copy(basis, first, first_sem)
    get_basis.start()
    copies = []
    for n in range(BATCHES):
        span = pl.ds(n * BATCH, BATCH)
        copies.append(pltpu.make_async_copy(tiles.at[span], stock.at[span], sems.at[n]))
        copies[-1].start()
    core, count = turn[0], live[0]

    def window(s):
        col = col_blocks[s]
        quarter = col // (CB // 4)
        position = (((quarter % 2) ^ core) * 2 + quarter // 2) * (CB // 4) + col % (CB // 4)
        return (
            pl.ds(pl.multiple_of(row_blocks[s] * TILE, TILE), TILE),
            pl.ds(pl.multiple_of(position * TILE, TILE), TILE),
        )

    def put(s, carry):
        dense[window(s)] = stock[s]
        return carry

    def clear(s, carry):
        dense[window(s)] = jnp.zeros((TILE, TILE), bf16)
        return carry

    for n in range(BATCHES):
        copies[n].wait()
        middle = jnp.clip(count, n * BATCH, (n + 1) * BATCH)
        lax.fori_loop(n * BATCH, middle, put, 0)
        lax.fori_loop(middle, (n + 1) * BATCH, clear, 0)
    get_basis.wait()
    image = jnp.zeros((K, HEIGHT), f32)
    for p in range(4):
        q = (p % 2) * 2 + ((p // 2) ^ core)
        part = first[:, pl.ds(pl.multiple_of(q * OWN, OWN), OWN)]
        image = image + dot_rows(part, dense[:, p * OWN : (p + 1) * OWN])
    write_packed(packed, image, None)


def gathered(chunk, mine, other, dense):
    image, grams = 0.0, []
    for p, half in ((chunk, mine), (2 + chunk, other)):
        parts = two_parts(half[...])
        grams.append(gram_of(parts))
        image = image + dot_rows(parts, dense[:, p * OWN : (p + 1) * OWN])
    return image[:K] + image[K:], grams[0] + grams[1]


def forward_kernel(mine, other, dense, image, gram):
    image[...], gram[...] = gathered(0, mine, other, dense)


def forward_last_kernel(mine, other, dense, image_before, gram_before, packed):
    image, gram = gathered(1, mine, other, dense)
    gram = gram_before[...] + gram
    write_packed(packed, image_before[...] + image, jnp.concatenate([gram, gram], axis=1))


def gram_kernel(own, out):
    gram = gram_of(two_parts(own[...]))
    out[...] = jnp.concatenate([gram[: K // 2], gram[K // 2 :]], axis=1)


def image_of(packed):
    return jnp.concatenate(
        [jnp.concatenate([read_packed(packed, g * 8 + j) for j in range(8)], axis=1) for g in range(8)],
        axis=0,
    )


def spread(chunk, image_half, dense, mine, other):
    for p, target in ((chunk, mine), (2 + chunk, other)):
        for n in range(2):
            width = OWN // 2
            source = pl.ds(p * OWN + n * width, width)
            product = jnp.dot(image_half, dense[:, source], preferred_element_type=f32)
            target[:, n * width : (n + 1) * width] = product


def first_backward_kernel(packed, dense, mine, other, kept):
    kept[...] = image_of(packed).astype(bf16)
    spread(0, kept[...], dense, mine, other)


def backward_kernel(packed, dense, mine, other, kept, inverse):
    gram = jnp.concatenate([read_packed(packed, 64 + g) for g in range(8)], axis=0)[:, :K]
    found = inverse_factor(gram * (1.0 / CELLS))
    inverse[...] = found
    image = jnp.dot(found, image_of(packed), precision=lax.Precision.HIGHEST, preferred_element_type=f32)
    kept[...] = image.astype(bf16)
    spread(0, kept[...], dense, mine, other)


def backward_last_kernel(kept, dense, mine, other):
    spread(1, kept[...], dense, mine, other)


def add_kernel(a, b, out):
    out[...] = a[...] + b[...]


def share_kernel(parts, out):
    total = parts[0]
    for n in range(1, parts.shape[0]):
        total = total + parts[n]
    for n in range(out.shape[0]):
        out[n] = total


def finish_kernel(turn, gram, *refs):
    halves, last_half, inverses, out = refs[: 2 * ITERS - 2], refs[2 * ITERS - 2], refs[2 * ITERS - 1 : -1], refs[-1]
    whole = jnp.concatenate([gram[:, :K], gram[:, K:]], axis=0)
    last = inverse_factor(whole * (1.0 / CELLS))
    for i in range(ITERS):
        if i < ITERS - 1:
            found, taken = inverses[i][...], jnp.where(turn[1] == 0, halves[2 * i][...], halves[2 * i + 1][...])
        else:
            found, taken = last, last_half[...]
        out[i] = jnp.dot(found, taken, precision=lax.Precision.HIGHEST, preferred_element_type=f32)


def shifted(x, axis, by):
    count = lax.axis_size(axis)
    return lax.ppermute(x, axis, [(i, (i + by) % count) for i in range(count)])


def summed_by_all(x, axes):
    count = lax.axis_size(axes)
    return jnp.sum(lax.all_to_all(jnp.broadcast_to(x[None], (count, *x.shape)), axes, 0, 0, tiled=True), axis=0)


def call(kernel, name, mib, ins, outs, arrays, flops=0, scratch=()):
    shapes = tuple(jax.ShapeDtypeStruct(*o) for o in outs)
    moved = sum(a.size * a.dtype.itemsize for a in (*arrays, *shapes))
    found = pl.pallas_call(
        kernel,
        out_shape=shapes,
        in_specs=ins,
        out_specs=(VMEM,) * len(outs),
        scratch_shapes=list(scratch),
        compiler_params=params(mib),
        cost_estimate=pl.CostEstimate(flops=flops, bytes_accessed=moved, transcendentals=0),
        name=name,
    )(*arrays)
    return found[0] if len(outs) == 1 else found


def shared(parts, count):
    return call(share_kernel, "share", 4, [VMEM], [((count, *parts.shape[1:]), f32)], [parts])


def added(a, b):
    return call(add_kernel, "add", 4, [VMEM, VMEM], [(a.shape, f32)], [a, b])


def summed_over_blk(packed):
    shares = lax.all_to_all(packed, PLANE, 0, 0, tiled=True)
    shares = lax.all_to_all(shared(shares, 4), "h", 0, 0, tiled=True)
    return lax.all_to_all(shared(shares, PEERS), PLANE, 0, 0, tiled=True)


def local(sens_tiles, start_basis, row_blocks, col_blocks, live_counts):
    core, low = lax.axis_index("c"), lax.axis_index("l")
    turn = jnp.stack([core, low]).astype(jnp.int32)
    packed_shape = ((PEERS, EACH * 8, TILE), f32)
    chunk, square, kept_shape = ((K, OWN), f32), ((K, K), f32), ((K, HEIGHT), bf16)
    work = 2 * K * HEIGHT * HALF
    dense, packed = call(
        start_kernel,
        "start",
        START_MIB,
        [SMEM, SMEM, SMEM, SMEM, HBM, HBM],
        [((HEIGHT, WIDTH), bf16), packed_shape],
        [row_blocks.reshape(MAXB), col_blocks.reshape(MAXB), live_counts.reshape(1), turn, sens_tiles, start_basis],
        2 * work,
        [
            pltpu.VMEM(sens_tiles.shape, bf16),
            pltpu.VMEM(start_basis.shape, bf16),
            pltpu.SemaphoreType.DMA((BATCHES,)),
            pltpu.SemaphoreType.DMA,
        ],
    )
    halves, inverses = [], []
    for iteration in range(ITERS):
        packed = summed_over_blk(packed)
        if iteration == 0:
            mine, other, kept = call(first_backward_kernel, "backward", 8, [VMEM, VMEM], [chunk, chunk, kept_shape], [packed, dense], work)
        else:
            mine, other, kept, inverse = call(
                backward_kernel, "backward", 8, [VMEM, VMEM], [chunk, chunk, kept_shape, square], [packed, dense], work
            )
            inverses.append(inverse)
        moving = shifted(other, "c", 1)
        mine_last, other_last = call(backward_last_kernel, "backward_last", 8, [VMEM, VMEM], [chunk, chunk], [kept, dense], work)
        mine = added(mine, moving)
        if iteration == ITERS - 1:
            mine_last = added(mine_last, shifted(other_last, "c", 1))
            own = jnp.where(low == 0, mine, mine_last)
            sent = jnp.where(low == 0, mine_last, mine)
            own = own + shifted(sent, "l", 1)
            break
        moving = shifted(mine, "l", 1)
        mine_last = added(mine_last, shifted(other_last, "c", 1))
        moving_last = shifted(mine_last, "l", 1)
        mine, mine_last = lax.optimization_barrier((mine, mine_last))
        mine = added(mine, moving)
        image, gram = call(
            forward_kernel, "forward", 12, [VMEM, VMEM, VMEM], [chunk, square], [mine, shifted(mine, "c", 1), dense], 2 * work
        )
        mine_last = added(mine_last, moving_last)
        packed = call(
            forward_last_kernel,
            "forward_last",
            12,
            [VMEM] * 5,
            [packed_shape],
            [mine_last, shifted(mine_last, "c", 1), dense, image, gram],
            2 * work,
        )
        halves += [mine, mine_last]
    gram = call(gram_kernel, "gram", 50, [VMEM], [((K // 2, 2 * K), f32)], [own])
    gram = summed_by_all(summed_by_all(gram, PLANE + ("c",)), ("h", "l"))
    return call(
        finish_kernel,
        "finish",
        50,
        [SMEM] + [VMEM] * (3 * ITERS - 1),
        [((ITERS, K, OWN), f32)],
        [turn, gram, *halves, own, *inverses],
    )


def solution(mesh):
    fine = Mesh(mesh.devices.reshape(4, 4, 4, 2, 2), BLK + ROWS)
    in_specs = (
        P(BLK, ROWS, None),
        P(None, BLK),
        P(BLK, ROWS),
        P(BLK, ROWS),
        P(BLK, ROWS),
    )
    out_specs = P(None, None, BLK + ROWS)
    return jax.shard_map(local, mesh=fine, in_specs=in_specs, out_specs=out_specs, check_vma=False)
```

time: 305 us -> 282 us (0.925)
  waiting for transfers between devices: 60 us -> 44 us
  Pallas kernels: 59.8 us -> 43.9 us
  starting transfers between devices: 4.66 us -> 11.4 us
    all_to_all x4 -> x8, blocking collectives: 47.6 us -> 96.3 us  [the longest x4 48.7 us: summed_over_blk(): shares = lax.all_to_all(shared(shares, 4), 'h', 0, 0, tiled=True)]
    all_to_all x6 -> x2, blocking collectives: 75.8 us -> 27.1 us  [summed_by_all(): lax.all_to_all(jnp.broadcast_to(x[None], (count, *x.shape)), axes, 0, 0,...]
    ppermute x11 -> x21, waiting for transfers between devices: 60 us -> 44 us  [shifted(): return lax.ppermute(x, axis, [(i, (i + by) % count) for i in range(count)])]
    pallas_call x10 -> x39, Pallas kernels: 59.8 us -> 43.9 us  [call(): pl.pallas_call(kernel, out_shape=shapes, in_specs=ins, out_specs=(VMEM,)...]
    ppermute x11 -> x21, starting transfers between devices: 4.66 us -> 11.4 us  [shifted(): return lax.ppermute(x, axis, [(i, (i + by) % count) for i in range(count)])]
  transfers between devices with their start and end apart: 11 -> 21, of which waited for: 11 -> 12; matrix products, arithmetic and copies ran while one was open for 0% -> 0% of each run, Pallas kernels for 0% -> 3%
where the time goes in v1:
time: 282 us; the launch traced here: 281 us
  blocking collectives  177 us (63%)
  waiting for transfers between devices  44 us (16%)
  Pallas kernels  43.9 us (16%)
  starting transfers between devices  11.4 us (4%)
    all_to_all x4, blocking collectives, summed_over_blk(): shares = lax.all_to_all(packed, PLANE, 0, 0, tiled=True)  54.1 us
    all_to_all x4, blocking collectives, summed_over_blk(): shares = lax.all_to_all(shared(shares, 4), 'h', 0, 0, tiled=True)  48.7 us
    all_to_all x4, blocking collectives, summed_over_blk(): return lax.all_to_all(shared(shares, PEERS), PLANE, 0, 0, tiled=True)  47.6 us
    ppermute x21, waiting for transfers between devices, shifted(): return lax.ppermute(x, axis, [(i, (i + by) % count) for i in range(count)])  44 us
    pallas_call x39, Pallas kernels, call(): pl.pallas_call(kernel, out_shape=shapes, in_specs=ins, out_specs=(VMEM,)...  43.9 us
    all_to_all x2, blocking collectives, summed_by_all(): lax.all_to_all(jnp.broadcast_to(x[None], (count, *x.shape)), axes, 0, 0,...  27.1 us
    ppermute x21, starting transfers between devices, shifted(): return lax.ppermute(x, axis, [(i, (i + by) % count) for i in range(count)])  11.4 us
  transfers between devices with their start and end apart: 21, of which 12 were waited for; matrix products, arithmetic and copies ran while one was open for 0% of the time, Pallas kernels for 3%

profile of v1, /device:TPU:2, one launch (start us, length us, event | category | flops | bytes accessed | tf_op | source)
XLA Modules:
  0.0 280.5 jit_solution(891242704122509156)
XLA Ops:
  3.1 10.9 %start.1 = (bf16[1024,4096]{1,0:T(8,128)(2,1)S(1)}, f32[16,40,128]{2,1,0:T(8,128)S(1)}) custom-call(s32[256]{0:T(256)S(1)} %bitcast.6, s32[256]{0:T(256)S(1)} %bitcast.7, s32[1]{0:T(128)} %bitcast.5.live, s32[2]{0:T(128)S(1)} %pad_add_fusion.turn, bf16[256,128,128]{2,1,0:T(8,128)(2,1)} %tiles.1, bf16[64,4096]{1,0:T(8,128)(2,1)S(1)} %copy-done), custom_call_target="tpu_custom_call" | custom-call | flops 536870912 | bytes 17631244 | tf_op jit(solution)/shard_map/start/pallas_call | solution.py:237
  14.1 15.3 %all_to_all.70.parts = f32[16,40,128]{2,1,0:T(8,128)S(1)} all-to-all(f32[16,40,128]{2,1,0:T(8,128)S(1)} %get-tuple-element.42), channel_id=1, replica_groups=mesh['y'=4,'x'=4,'h'=4,'l'=2,'c'=2] {'y','x'}, dimensions={0} | all-to-all | bytes 655360 | tf_op jit(solution)/shard_map/all_to_all | solution.py:259
  29.4 16.6 %all_to_all.71.parts = f32[4,40,128]{2,1,0:T(8,128)S(1)} all-to-all(f32[4,40,128]{2,1,0:T(8,128)S(1)} %share.8), channel_id=1, replica_groups=mesh['y'=4,'x'=4,'h'=4,'l'=2,'c'=2] {'h'}, dimensions={0} | all-to-all | bytes 163840 | tf_op jit(solution)/shard_map/all_to_all | solution.py:260
  46.0 11.9 %all_to_all.72.packed = f32[16,40,128]{2,1,0:T(8,128)S(1)} all-to-all(f32[16,40,128]{2,1,0:T(8,128)S(1)} %share.9), channel_id=1, replica_groups=mesh['y'=4,'x'=4,'h'=4,'l'=2,'c'=2] {'y','x'}, dimensions={0} | all-to-all | bytes 655360 | tf_op jit(solution)/shard_map/all_to_all | solution.py:261
  62.7 7.0 %collective-permute-done.4.b = f32[64,1024]{1,0:T(8,128)S(1)} collective-permute-done((f32[64,1024]{1,0:T(8,128)S(1)}, f32[64,1024]{1,0:T(8,128)S(1)}, u32[]{:S(2)}, u32[]{:S(2)}) %collective-permute-start.4) | collective-permute-done | bytes 262176 | tf_op jit(solution)/shard_map/ppermute | solution.py:226
  69.8 4.7 %collective-permute-done.2.b = f32[64,1024]{1,0:T(8,128)S(1)} collective-permute-done((f32[64,1024]{1,0:T(8,128)S(1)}, f32[64,1024]{1,0:T(8,128)S(1)}, u32[]{:S(2)}, u32[]{:S(2)}) %collective-permute-start.2) | collective-permute-done | bytes 262176 | tf_op jit(solution)/shard_map/ppermute | solution.py:226
  78.0 12.9 %all_to_all.73.parts = f32[16,40,128]{2,1,0:T(8,128)S(1)} all-to-all(f32[16,40,128]{2,1,0:T(8,128)S(1)} %forward_last.3), channel_id=1, replica_groups=mesh['y'=4,'x'=4,'h'=4,'l'=2,'c'=2] {'y','x'}, dimensions={0} | all-to-all | bytes 655360 | tf_op jit(solution)/shard_map/all_to_all | solution.py:259
  90.9 10.7 %all_to_all.74.parts = f32[4,40,128]{2,1,0:T(8,128)S(1)} all-to-all(f32[4,40,128]{2,1,0:T(8,128)S(1)} %share.10), channel_id=1, replica_groups=mesh['y'=4,'x'=4,'h'=4,'l'=2,'c'=2] {'h'}, dimensions={0} | all-to-all | bytes 163840 | tf_op jit(solution)/shard_map/all_to_all | solution.py:260
  101.7 11.9 %all_to_all.75.packed = f32[16,40,128]{2,1,0:T(8,128)S(1)} all-to-all(f32[16,40,128]{2,1,0:T(8,128)S(1)} %share.11), channel_id=1, replica_groups=mesh['y'=4,'x'=4,'h'=4,'l'=2,'c'=2] {'y','x'}, dimensions={0} | all-to-all | bytes 655360 | tf_op jit(solution)/shard_map/all_to_all | solution.py:261
  121.9 7.0 %collective-permute-done.10.b = f32[64,1024]{1,0:T(8,128)S(1)} collective-permute-done((f32[64,1024]{1,0:T(8,128)S(1)}, f32[64,1024]{1,0:T(8,128)S(1)}, u32[]{:S(2)}, u32[]{:S(2)}) %collective-permute-start.10) | collective-permute-done | bytes 262176 | tf_op jit(solution)/shard_map/ppermute | solution.py:226
  129.0 4.7 %collective-permute-done.8.b = f32[64,1024]{1,0:T(8,128)S(1)} collective-permute-done((f32[64,1024]{1,0:T(8,128)S(1)}, f32[64,1024]{1,0:T(8,128)S(1)}, u32[]{:S(2)}, u32[]{:S(2)}) %collective-permute-start.8) | collective-permute-done | bytes 262176 | tf_op jit(solution)/shard_map/ppermute | solution.py:226
  137.2 12.9 %all_to_all.76.parts = f32[16,40,128]{2,1,0:T(8,128)S(1)} all-to-all(f32[16,40,128]{2,1,0:T(8,128)S(1)} %forward_last.4), channel_id=1, replica_groups=mesh['y'=4,'x'=4,'h'=4,'l'=2,'c'=2] {'y','x'}, dimensions={0} | all-to-all | bytes 655360 | tf_op jit(solution)/shard_map/all_to_all | solution.py:259
  150.2 10.7 %all_to_all.77.parts = f32[4,40,128]{2,1,0:T(8,128)S(1)} all-to-all(f32[4,40,128]{2,1,0:T(8,128)S(1)} %share.12), channel_id=1, replica_groups=mesh['y'=4,'x'=4,'h'=4,'l'=2,'c'=2] {'h'}, dimensions={0} | all-to-all | bytes 163840 | tf_op jit(solution)/shard_map/all_to_all | solution.py:260
  160.9 11.9 %all_to_all.78.packed = f32[16,40,128]{2,1,0:T(8,128)S(1)} all-to-all(f32[16,40,128]{2,1,0:T(8,128)S(1)} %share.13), channel_id=1, replica_groups=mesh['y'=4,'x'=4,'h'=4,'l'=2,'c'=2] {'y','x'}, dimensions={0} | all-to-all | bytes 655360 | tf_op jit(solution)/shard_map/all_to_all | solution.py:261
  172.8 4.2 %backward.6 = (f32[64,1024]{1,0:T(8,128)S(1)}, f32[64,1024]{1,0:T(8,128)S(1)}, bf16[64,1024]{1,0:T(8,128)(2,1)S(1)}, f32[64,64]{1,0:T(8,128)S(1)}) custom-call(f32[16,40,128]{2,1,0:T(8,128)S(1)} %all_to_all.78.packed, bf16[1024,4096]{1,0:T(8,128)(2,1)S(1)} %get-tuple-element.43.dense), custom_call_target="tpu_custom_call" | custom-call | flops 268435456 | bytes 9388032 | tf_op jit(solution)/shard_map/backward/pallas_call | solution.py:237
  180.9 7.0 %collective-permute-done.16.b = f32[64,1024]{1,0:T(8,128)S(1)} collective-permute-done((f32[64,1024]{1,0:T(8,128)S(1)}, f32[64,1024]{1,0:T(8,128)S(1)}, u32[]{:S(2)}, u32[]{:S(2)}) %collective-permute-start.16) | collective-permute-done | bytes 262176 | tf_op jit(solution)/shard_map/ppermute | solution.py:226
  188.1 4.7 %collective-permute-done.14.b = f32[64,1024]{1,0:T(8,128)S(1)} collective-permute-done((f32[64,1024]{1,0:T(8,128)S(1)}, f32[64,1024]{1,0:T(8,128)S(1)}, u32[]{:S(2)}, u32[]{:S(2)}) %collective-permute-start.14) | collective-permute-done | bytes 262176 | tf_op jit(solution)/shard_map/ppermute | solution.py:226
  196.5 12.9 %all_to_all.79.parts = f32[16,40,128]{2,1,0:T(8,128)S(1)} all-to-all(f32[16,40,128]{2,1,0:T(8,128)S(1)} %forward_last.5), channel_id=1, replica_groups=mesh['y'=4,'x'=4,'h'=4,'l'=2,'c'=2] {'y','x'}, dimensions={0} | all-to-all | bytes 655360 | tf_op jit(solution)/shard_map/all_to_all | solution.py:259
  209.4 10.7 %all_to_all.80.parts = f32[4,40,128]{2,1,0:T(8,128)S(1)} all-to-all(f32[4,40,128]{2,1,0:T(8,128)S(1)} %share.14), channel_id=1, replica_groups=mesh['y'=4,'x'=4,'h'=4,'l'=2,'c'=2] {'h'}, dimensions={0} | all-to-all | bytes 163840 | tf_op jit(solution)/shard_map/all_to_all | solution.py:260
  220.2 11.9 %all_to_all.81.packed = f32[16,40,128]{2,1,0:T(8,128)S(1)} all-to-all(f32[16,40,128]{2,1,0:T(8,128)S(1)} %share.15), channel_id=1, replica_groups=mesh['y'=4,'x'=4,'h'=4,'l'=2,'c'=2] {'y','x'}, dimensions={0} | all-to-all | bytes 655360 | tf_op jit(solution)/shard_map/all_to_all | solution.py:261
  240.2 7.5 %collective-permute-done.20 = f32[64,1024]{1,0:T(8,128)S(1)} collective-permute-done((f32[64,1024]{1,0:T(8,128)S(1)}, f32[64,1024]{1,0:T(8,128)S(1)}, u32[]{:S(2)}, u32[]{:S(2)}) %collective-permute-start.20) | collective-permute-done | bytes 262176 | tf_op jit(solution)/shard_map/ppermute | solution.py:226
  248.2 14.9 %all_to_all.82 = f32[32,32,128]{2,1,0:T(8,128)S(1)} all-to-all(f32[32,32,128]{2,1,0:T(8,128)S(1)} %broadcast_in_dim.4), channel_id=1, replica_groups=mesh['y'=4,'x'=4,'h'=4,'l'=2,'c'=2] {'y','x','c'}, dimensions={0} | all-to-all | bytes 1048576 | tf_op jit(solution)/shard_map/all_to_all | solution.py:231
  263.1 12.3 %all_to_all.83 = f32[8,32,128]{2,1,0:T(8,128)S(1)} all-to-all(f32[8,32,128]{2,1,0:T(8,128)S(1)} %broadcast_in_dim.5), channel_id=1, replica_groups=mesh['y'=4,'x'=4,'h'=4,'l'=2,'c'=2] {'h','l'}, dimensions={0} | all-to-all | bytes 262144 | tf_op jit(solution)/shard_map/all_to_all | solution.py:231
  275.4 5.1 %finish.1 = f32[4,64,1024]{2,1,0:T(8,128)} custom-call(s32[2]{0:T(128)S(1)} %pad_add_fusion.turn, f32[32,128]{1,0:T(8,128)S(1)} %reduce_sum.19.gram, f32[64,1024]{1,0:T(8,128)S(1)} %add.24.mine.refs_0_, f32[64,1024]{1,0:T(8,128)S(1)} %add.23.mine.refs_1_, f32[64,1024]{1,0:T(8,128)S(1)} %add.28.mine.refs_2_, f32[64,1024]{1,0:T(8,128)S(1)} %add.27.mine.refs_3_, ...), custom_call_target="tpu_custom_call" | custom-call | bytes 2949128 | tf_op jit(solution)/shard_map/finish/pallas_call | solution.py:237
  (84 shorter events, 39.2 us)
Async XLA Ops:
  0.7 1.0 copy-start
  1.8 0.7 copy-start.1
  2.5 0.7 copy-start.2
  58.8 1.6 collective-permute-start
  59.7 1.8 collective-permute-start.1
  60.4 9.2 %collective-permute-start.4 = (f32[64,1024]{1,0:T(8,128)S(1)}, f32[64,1024]{1,0:T(8,128)S(1)}, u32[]{:S(2)}, u32[]{:S(2)}) collective-permute-start(f32[64,1024]{1,0:T(8,128)S(1)} %add.21.a), channel_id=1, source_target_pairs={{0,2},{2,0},{1,3},{3,1},{4,6},{6,4},{5,7},{7,5},{8,10},{10,8},{9,1... | collective-permute-start | bytes 786440 | tf_op jit(solution)/shard_map/ppermute | solution.py:226
  61.6 12.9 %collective-permute-start.2 = (f32[64,1024]{1,0:T(8,128)S(1)}, f32[64,1024]{1,0:T(8,128)S(1)}, u32[]{:S(2)}, u32[]{:S(2)}) collective-permute-start(f32[64,1024]{1,0:T(8,128)S(1)} %add.22.a), channel_id=1, source_target_pairs={{0,2},{2,0},{1,3},{3,1},{4,6},{6,4},{5,7},{7,5},{8,10},{10,8},{9,1... | collective-permute-start | bytes 786440 | tf_op jit(solution)/shard_map/ppermute | solution.py:226
  69.7 4.9 %collective-permute-start.5 = (f32[64,1024]{1,0:T(8,128)S(1)}, f32[64,1024]{1,0:T(8,128)S(1)}, u32[]{:S(2)}, u32[]{:S(2)}) collective-permute-start(f32[64,1024]{1,0:T(8,128)S(1)} %add.24.mine.refs_0_), channel_id=1, source_target_pairs={{0,1},{1,0},{2,3},{3,2},{4,5},{5,4},{6,7},{7,6},{8,9},{9,8},{10,11... | collective-permute-start | bytes 786440 | tf_op jit(solution)/shard_map/ppermute | solution.py:226
  74.5 1.8 collective-permute-start.3
  117.8 1.8 collective-permute-start.6
  118.9 1.8 collective-permute-start.7
  119.6 9.2 %collective-permute-start.10 = (f32[64,1024]{1,0:T(8,128)S(1)}, f32[64,1024]{1,0:T(8,128)S(1)}, u32[]{:S(2)}, u32[]{:S(2)}) collective-permute-start(f32[64,1024]{1,0:T(8,128)S(1)} %add.25.a), channel_id=1, source_target_pairs={{0,2},{2,0},{1,3},{3,1},{4,6},{6,4},{5,7},{7,5},{8,10},{10,8},{9,1... | collective-permute-start | bytes 786440 | tf_op jit(solution)/shard_map/ppermute | solution.py:226
  120.8 12.9 %collective-permute-start.8 = (f32[64,1024]{1,0:T(8,128)S(1)}, f32[64,1024]{1,0:T(8,128)S(1)}, u32[]{:S(2)}, u32[]{:S(2)}) collective-permute-start(f32[64,1024]{1,0:T(8,128)S(1)} %add.26.a), channel_id=1, source_target_pairs={{0,2},{2,0},{1,3},{3,1},{4,6},{6,4},{5,7},{7,5},{8,10},{10,8},{9,1... | collective-permute-start | bytes 786440 | tf_op jit(solution)/shard_map/ppermute | solution.py:226
  128.9 4.9 %collective-permute-start.11 = (f32[64,1024]{1,0:T(8,128)S(1)}, f32[64,1024]{1,0:T(8,128)S(1)}, u32[]{:S(2)}, u32[]{:S(2)}) collective-permute-start(f32[64,1024]{1,0:T(8,128)S(1)} %add.28.mine.refs_2_), channel_id=1, source_target_pairs={{0,1},{1,0},{2,3},{3,2},{4,5},{5,4},{6,7},{7,6},{8,9},{9,8},{10,11... | collective-permute-start | bytes 786440 | tf_op jit(solution)/shard_map/ppermute | solution.py:226
  133.7 1.8 collective-permute-start.9
  177.0 1.6 collective-permute-start.12
  178.0 1.8 collective-permute-start.13
  178.7 9.2 %collective-permute-start.16 = (f32[64,1024]{1,0:T(8,128)S(1)}, f32[64,1024]{1,0:T(8,128)S(1)}, u32[]{:S(2)}, u32[]{:S(2)}) collective-permute-start(f32[64,1024]{1,0:T(8,128)S(1)} %add.29.a), channel_id=1, source_target_pairs={{0,2},{2,0},{1,3},{3,1},{4,6},{6,4},{5,7},{7,5},{8,10},{10,8},{9,1... | collective-permute-start | bytes 786440 | tf_op jit(solution)/shard_map/ppermute | solution.py:226
  179.8 12.9 %collective-permute-start.14 = (f32[64,1024]{1,0:T(8,128)S(1)}, f32[64,1024]{1,0:T(8,128)S(1)}, u32[]{:S(2)}, u32[]{:S(2)}) collective-permute-start(f32[64,1024]{1,0:T(8,128)S(1)} %add.30.a), channel_id=1, source_target_pairs={{0,2},{2,0},{1,3},{3,1},{4,6},{6,4},{5,7},{7,5},{8,10},{10,8},{9,1... | collective-permute-start | bytes 786440 | tf_op jit(solution)/shard_map/ppermute | solution.py:226
  188.0 5.1 %collective-permute-start.17 = (f32[64,1024]{1,0:T(8,128)S(1)}, f32[64,1024]{1,0:T(8,128)S(1)}, u32[]{:S(2)}, u32[]{:S(2)}) collective-permute-start(f32[64,1024]{1,0:T(8,128)S(1)} %add.32.mine.refs_4_), channel_id=1, source_target_pairs={{0,1},{1,0},{2,3},{3,2},{4,5},{5,4},{6,7},{7,6},{8,9},{9,8},{10,11... | collective-permute-start | bytes 786440 | tf_op jit(solution)/shard_map/ppermute | solution.py:226
  192.8 2.0 collective-permute-start.15
  236.3 1.6 collective-permute-start.18
  237.2 1.7 collective-permute-start.19
  239.1 8.7 %collective-permute-start.20 = (f32[64,1024]{1,0:T(8,128)S(1)}, f32[64,1024]{1,0:T(8,128)S(1)}, u32[]{:S(2)}, u32[]{:S(2)}) collective-permute-start(f32[64,1024]{1,0:T(8,128)S(1)} %broadcast_select_fusion), channel_id=1, source_target_pairs={{0,2},{2,0},{1,3},{3,1},{4,6},{6,4},{5,7},{7,5},{8,10},{10,8},{9,1... | collective-permute-start | bytes 786440 | tf_op jit(solution)/shard_map/ppermute | solution.py:226

commit v2 on v1

--- a/solution.py
+++ b/solution.py
@@ -19,7 +19,7 @@
 OWN = WIDTH // 4
 PEERS = 16
 EACH = 5
-PANEL = 4
+PANEL = 8
 START_MIB = 40
 BATCHES = 8
 BATCH = MAXB // BATCHES
@@ -81,19 +81,23 @@
     shape = (K, 2 * K)
     row = lax.broadcasted_iota(jnp.int32, shape, 0)
     col = lax.broadcasted_iota(jnp.int32, shape, 1)
-    work = jnp.concatenate([gram, (row[:, :K] == col[:, :K]).astype(f32)], axis=1)
+    rest = jnp.concatenate([gram, (row[:, :K] == col[:, :K]).astype(f32)], axis=1)
+    finished = []
     for k in range(0, K, PANEL):
-        columns = [jnp.broadcast_to(work[:, k + j : k + j + 1], shape) for j in range(PANEL)]
-        lines = [work[k + j : k + j + 1, :] for j in range(PANEL)]
+        here = (K - k, 2 * K)
+        below = row[: K - k]
+        columns = [jnp.broadcast_to(rest[:, k + j : k + j + 1], here) for j in range(PANEL)]
+        lines = [rest[j : j + 1, :] for j in range(PANEL)]
         for j in range(PANEL):
-            at = k + j
-            inverse = reciprocal(columns[j][at : at + 1, :])
-            factor = jnp.where(row > at, columns[j] * inverse, 0.0)
+            inverse = reciprocal(columns[j][j : j + 1, :])
+            factor = jnp.where(below > j, columns[j] * inverse, 0.0)
             for later in range(j + 1, PANEL):
-                columns[later] = columns[later] - factor * columns[later][at : at + 1, :]
-                to = k + later
-                lines[later] = lines[later] - factor[to : to + 1, :] * lines[j]
-            work = work - factor * lines[j]
+                columns[later] = columns[later] - factor * columns[later][j : j + 1, :]
+                lines[later] = lines[later] - factor[later : later + 1, :] * lines[j]
+            rest = rest - factor * lines[j]
+        finished.append(rest[:PANEL])
+        rest = rest[PANEL:]
+    work = jnp.concatenate(finished, axis=0)
     diagonal = jnp.sum(jnp.where(row == col, work, 0.0), axis=1, keepdims=True)
     return work[:, K:] * lax.rsqrt(diagonal)
 
@@ -118,18 +122,12 @@
         )
 
     def put(s, carry):
-        dense[window(s)] = stock[s]
-        return carry
-
-    def clear(s, carry):
-        dense[window(s)] = jnp.zeros((TILE, TILE), bf16)
+        dense[window(s)] = jnp.where(s < count, stock[s], jnp.zeros((TILE, TILE), bf16))
         return carry
 
     for n in range(BATCHES):
         copies[n].wait()
-        middle = jnp.clip(count, n * BATCH, (n + 1) * BATCH)
-        lax.fori_loop(n * BATCH, middle, put, 0)
-        lax.fori_loop(middle, (n + 1) * BATCH, clear, 0)
+        lax.fori_loop(n * BATCH, (n + 1) * BATCH, put, 0, unroll=8)
     get_basis.wait()
     image = jnp.zeros((K, HEIGHT), f32)
     for p in range(4):
@@ -321,7 +319,7 @@
         )
         halves += [mine, mine_last]
     gram = call(gram_kernel, "gram", 50, [VMEM], [((K // 2, 2 * K), f32)], [own])
-    gram = summed_by_all(summed_by_all(gram, PLANE + ("c",)), ("h", "l"))
+    gram = summed_by_all(summed_by_all(gram + shifted(gram, "c", 1), PLANE), ("h", "l"))
     return call(
         finish_kernel,
         "finish",

time: 282 us -> 274 us (0.972)
  Pallas kernels: 43.9 us -> 40.1 us
  blocking collectives: 177 us -> 174 us
    pallas_call x39, Pallas kernels: 43.9 us -> 40.1 us  [call(): pl.pallas_call(kernel, out_shape=shapes, in_specs=ins, out_specs=(VMEM,)...]
    all_to_all x2, blocking collectives: 27.1 us -> 23.4 us  [summed_by_all(): lax.all_to_all(jnp.broadcast_to(x[None], (count, *x.shape)), axes, 0, 0,...]
    ppermute x21 -> x22, waiting for transfers between devices: 44 us -> 45 us  [shifted(): return lax.ppermute(x, axis, [(i, (i + by) % count) for i in range(count)])]
    ppermute x21 -> x22, starting transfers between devices: 11.4 us -> 11.3 us  [shifted(): return lax.ppermute(x, axis, [(i, (i + by) % count) for i in range(count)])]
  transfers between devices with their start and end apart: 21 -> 22, of which waited for: 12 -> 12; matrix products, arithmetic and copies ran while one was open for 0% -> 0% of each run, Pallas kernels for 3% -> 3%
where the time goes in v2:
time: 274 us
  blocking collectives  174 us (64%)
  waiting for transfers between devices  45 us (16%)
  Pallas kernels  40.1 us (15%)
  starting transfers between devices  11.3 us (4%)
    all_to_all x4, blocking collectives, summed_over_blk(): shares = lax.all_to_all(packed, PLANE, 0, 0, tiled=True)  54.1 us
    all_to_all x4, blocking collectives, summed_over_blk(): shares = lax.all_to_all(shared(shares, 4), 'h', 0, 0, tiled=True)  48.7 us
    all_to_all x4, blocking collectives, summed_over_blk(): return lax.all_to_all(shared(shares, PEERS), PLANE, 0, 0, tiled=True)  47.6 us
    ppermute x22, waiting for transfers between devices, shifted(): return lax.ppermute(x, axis, [(i, (i + by) % count) for i in range(count)])  45 us
    pallas_call x39, Pallas kernels, call(): pl.pallas_call(kernel, out_shape=shapes, in_specs=ins, out_specs=(VMEM,)...  40.1 us
    all_to_all x2, blocking collectives, summed_by_all(): lax.all_to_all(jnp.broadcast_to(x[None], (count, *x.shape)), axes, 0, 0,...  23.4 us
    ppermute x22, starting transfers between devices, shifted(): return lax.ppermute(x, axis, [(i, (i + by) % count) for i in range(count)])  11.3 us
  transfers between devices with their start and end apart: 22, of which 12 were waited for; matrix products, arithmetic and copies ran while one was open for 0% of the time, Pallas kernels for 3%

profile of v2, /device:TPU:2, one launch (start us, length us, event | category | flops | bytes accessed | tf_op | source)
XLA Modules:
  0.0 273.7 jit_solution(8955718388783725793)
XLA Ops:
  3.1 9.7 %start.1 = (bf16[1024,4096]{1,0:T(8,128)(2,1)S(1)}, f32[16,40,128]{2,1,0:T(8,128)S(1)}) custom-call(s32[256]{0:T(256)S(1)} %bitcast.6, s32[256]{0:T(256)S(1)} %bitcast.7, s32[1]{0:T(128)} %bitcast.5.live, s32[2]{0:T(128)S(1)} %pad_add_fusion.turn, bf16[256,128,128]{2,1,0:T(8,128)(2,1)} %tiles.1, bf16[64,4096]{1,0:T(8,128)(2,1)S(1)} %copy-done), custom_call_target="tpu_custom_call" | custom-call | flops 536870912 | bytes 17631244 | tf_op jit(solution)/shard_map/start/pallas_call | solution.py:235
  12.9 15.3 %all_to_all.70.parts = f32[16,40,128]{2,1,0:T(8,128)S(1)} all-to-all(f32[16,40,128]{2,1,0:T(8,128)S(1)} %get-tuple-element.42), channel_id=1, replica_groups=mesh['y'=4,'x'=4,'h'=4,'l'=2,'c'=2] {'y','x'}, dimensions={0} | all-to-all | bytes 655360 | tf_op jit(solution)/shard_map/all_to_all | solution.py:257
  28.2 16.6 %all_to_all.71.parts = f32[4,40,128]{2,1,0:T(8,128)S(1)} all-to-all(f32[4,40,128]{2,1,0:T(8,128)S(1)} %share.8), channel_id=1, replica_groups=mesh['y'=4,'x'=4,'h'=4,'l'=2,'c'=2] {'h'}, dimensions={0} | all-to-all | bytes 163840 | tf_op jit(solution)/shard_map/all_to_all | solution.py:258
  44.8 11.9 %all_to_all.72.packed = f32[16,40,128]{2,1,0:T(8,128)S(1)} all-to-all(f32[16,40,128]{2,1,0:T(8,128)S(1)} %share.9), channel_id=1, replica_groups=mesh['y'=4,'x'=4,'h'=4,'l'=2,'c'=2] {'y','x'}, dimensions={0} | all-to-all | bytes 655360 | tf_op jit(solution)/shard_map/all_to_all | solution.py:259
  61.4 7.0 %collective-permute-done.4.b = f32[64,1024]{1,0:T(8,128)S(1)} collective-permute-done((f32[64,1024]{1,0:T(8,128)S(1)}, f32[64,1024]{1,0:T(8,128)S(1)}, u32[]{:S(2)}, u32[]{:S(2)}) %collective-permute-start.4) | collective-permute-done | bytes 262176 | tf_op jit(solution)/shard_map/ppermute | solution.py:224
  68.6 4.7 %collective-permute-done.2.b = f32[64,1024]{1,0:T(8,128)S(1)} collective-permute-done((f32[64,1024]{1,0:T(8,128)S(1)}, f32[64,1024]{1,0:T(8,128)S(1)}, u32[]{:S(2)}, u32[]{:S(2)}) %collective-permute-start.2) | collective-permute-done | bytes 262176 | tf_op jit(solution)/shard_map/ppermute | solution.py:224
  76.8 12.9 %all_to_all.73.parts = f32[16,40,128]{2,1,0:T(8,128)S(1)} all-to-all(f32[16,40,128]{2,1,0:T(8,128)S(1)} %forward_last.3), channel_id=1, replica_groups=mesh['y'=4,'x'=4,'h'=4,'l'=2,'c'=2] {'y','x'}, dimensions={0} | all-to-all | bytes 655360 | tf_op jit(solution)/shard_map/all_to_all | solution.py:257
  89.7 10.7 %all_to_all.74.parts = f32[4,40,128]{2,1,0:T(8,128)S(1)} all-to-all(f32[4,40,128]{2,1,0:T(8,128)S(1)} %share.10), channel_id=1, replica_groups=mesh['y'=4,'x'=4,'h'=4,'l'=2,'c'=2] {'h'}, dimensions={0} | all-to-all | bytes 163840 | tf_op jit(solution)/shard_map/all_to_all | solution.py:258
  100.5 11.9 %all_to_all.75.packed = f32[16,40,128]{2,1,0:T(8,128)S(1)} all-to-all(f32[16,40,128]{2,1,0:T(8,128)S(1)} %share.11), channel_id=1, replica_groups=mesh['y'=4,'x'=4,'h'=4,'l'=2,'c'=2] {'y','x'}, dimensions={0} | all-to-all | bytes 655360 | tf_op jit(solution)/shard_map/all_to_all | solution.py:259
  112.4 3.6 %backward.5 = (f32[64,1024]{1,0:T(8,128)S(1)}, f32[64,1024]{1,0:T(8,128)S(1)}, bf16[64,1024]{1,0:T(8,128)(2,1)S(1)}, f32[64,64]{1,0:T(8,128)S(1)}) custom-call(f32[16,40,128]{2,1,0:T(8,128)S(1)} %all_to_all.75.packed, bf16[1024,4096]{1,0:T(8,128)(2,1)S(1)} %get-tuple-element.43.dense), custom_call_target="tpu_custom_call" | custom-call | flops 268435456 | bytes 9388032 | tf_op jit(solution)/shard_map/backward/pallas_call | solution.py:235
  119.8 7.0 %collective-permute-done.10.b = f32[64,1024]{1,0:T(8,128)S(1)} collective-permute-done((f32[64,1024]{1,0:T(8,128)S(1)}, f32[64,1024]{1,0:T(8,128)S(1)}, u32[]{:S(2)}, u32[]{:S(2)}) %collective-permute-start.10) | collective-permute-done | bytes 262176 | tf_op jit(solution)/shard_map/ppermute | solution.py:224
  127.0 4.7 %collective-permute-done.8.b = f32[64,1024]{1,0:T(8,128)S(1)} collective-permute-done((f32[64,1024]{1,0:T(8,128)S(1)}, f32[64,1024]{1,0:T(8,128)S(1)}, u32[]{:S(2)}, u32[]{:S(2)}) %collective-permute-start.8) | collective-permute-done | bytes 262176 | tf_op jit(solution)/shard_map/ppermute | solution.py:224
  135.1 12.9 %all_to_all.76.parts = f32[16,40,128]{2,1,0:T(8,128)S(1)} all-to-all(f32[16,40,128]{2,1,0:T(8,128)S(1)} %forward_last.4), channel_id=1, replica_groups=mesh['y'=4,'x'=4,'h'=4,'l'=2,'c'=2] {'y','x'}, dimensions={0} | all-to-all | bytes 655360 | tf_op jit(solution)/shard_map/all_to_all | solution.py:257
  148.1 10.7 %all_to_all.77.parts = f32[4,40,128]{2,1,0:T(8,128)S(1)} all-to-all(f32[4,40,128]{2,1,0:T(8,128)S(1)} %share.12), channel_id=1, replica_groups=mesh['y'=4,'x'=4,'h'=4,'l'=2,'c'=2] {'h'}, dimensions={0} | all-to-all | bytes 163840 | tf_op jit(solution)/shard_map/all_to_all | solution.py:258
  158.8 11.9 %all_to_all.78.packed = f32[16,40,128]{2,1,0:T(8,128)S(1)} all-to-all(f32[16,40,128]{2,1,0:T(8,128)S(1)} %share.13), channel_id=1, replica_groups=mesh['y'=4,'x'=4,'h'=4,'l'=2,'c'=2] {'y','x'}, dimensions={0} | all-to-all | bytes 655360 | tf_op jit(solution)/shard_map/all_to_all | solution.py:259
  178.4 7.0 %collective-permute-done.16.b = f32[64,1024]{1,0:T(8,128)S(1)} collective-permute-done((f32[64,1024]{1,0:T(8,128)S(1)}, f32[64,1024]{1,0:T(8,128)S(1)}, u32[]{:S(2)}, u32[]{:S(2)}) %collective-permute-start.16) | collective-permute-done | bytes 262176 | tf_op jit(solution)/shard_map/ppermute | solution.py:224
  185.5 4.6 %collective-permute-done.14.b = f32[64,1024]{1,0:T(8,128)S(1)} collective-permute-done((f32[64,1024]{1,0:T(8,128)S(1)}, f32[64,1024]{1,0:T(8,128)S(1)}, u32[]{:S(2)}, u32[]{:S(2)}) %collective-permute-start.14) | collective-permute-done | bytes 262176 | tf_op jit(solution)/shard_map/ppermute | solution.py:224
  193.5 12.9 %all_to_all.79.parts = f32[16,40,128]{2,1,0:T(8,128)S(1)} all-to-all(f32[16,40,128]{2,1,0:T(8,128)S(1)} %forward_last.5), channel_id=1, replica_groups=mesh['y'=4,'x'=4,'h'=4,'l'=2,'c'=2] {'y','x'}, dimensions={0} | all-to-all | bytes 655360 | tf_op jit(solution)/shard_map/all_to_all | solution.py:257
  206.5 10.7 %all_to_all.80.parts = f32[4,40,128]{2,1,0:T(8,128)S(1)} all-to-all(f32[4,40,128]{2,1,0:T(8,128)S(1)} %share.14), channel_id=1, replica_groups=mesh['y'=4,'x'=4,'h'=4,'l'=2,'c'=2] {'h'}, dimensions={0} | all-to-all | bytes 163840 | tf_op jit(solution)/shard_map/all_to_all | solution.py:258
  217.2 11.9 %all_to_all.81.packed = f32[16,40,128]{2,1,0:T(8,128)S(1)} all-to-all(f32[16,40,128]{2,1,0:T(8,128)S(1)} %share.15), channel_id=1, replica_groups=mesh['y'=4,'x'=4,'h'=4,'l'=2,'c'=2] {'y','x'}, dimensions={0} | all-to-all | bytes 655360 | tf_op jit(solution)/shard_map/all_to_all | solution.py:259
  236.6 7.6 %collective-permute-done.20 = f32[64,1024]{1,0:T(8,128)S(1)} collective-permute-done((f32[64,1024]{1,0:T(8,128)S(1)}, f32[64,1024]{1,0:T(8,128)S(1)}, u32[]{:S(2)}, u32[]{:S(2)}) %collective-permute-start.20) | collective-permute-done | bytes 262176 | tf_op jit(solution)/shard_map/ppermute | solution.py:224
  245.8 11.9 %all_to_all.82 = f32[16,32,128]{2,1,0:T(8,128)S(1)} all-to-all(f32[16,32,128]{2,1,0:T(8,128)S(1)} %broadcast_in_dim.4), channel_id=1, replica_groups=mesh['y'=4,'x'=4,'h'=4,'l'=2,'c'=2] {'y','x'}, dimensions={0} | all-to-all | bytes 524288 | tf_op jit(solution)/shard_map/all_to_all | solution.py:229
  257.7 11.5 %all_to_all.83 = f32[8,32,128]{2,1,0:T(8,128)S(1)} all-to-all(f32[8,32,128]{2,1,0:T(8,128)S(1)} %broadcast_in_dim.5), channel_id=1, replica_groups=mesh['y'=4,'x'=4,'h'=4,'l'=2,'c'=2] {'h','l'}, dimensions={0} | all-to-all | bytes 262144 | tf_op jit(solution)/shard_map/all_to_all | solution.py:229
  269.2 4.4 %finish.1 = f32[4,64,1024]{2,1,0:T(8,128)} custom-call(s32[2]{0:T(128)S(1)} %pad_add_fusion.turn, f32[32,128]{1,0:T(8,128)S(1)} %reduce_sum.19.gram, f32[64,1024]{1,0:T(8,128)S(1)} %add.28.mine.refs_0_, f32[64,1024]{1,0:T(8,128)S(1)} %add.27.mine.refs_1_, f32[64,1024]{1,0:T(8,128)S(1)} %add.32.mine.refs_2_, f32[64,1024]{1,0:T(8,128)S(1)} %add.31.mine.refs_3_, ...), custom_call_target="tpu_custom_call" | custom-call | bytes 2949128 | tf_op jit(solution)/shard_map/finish/pallas_call | solution.py:235
  (87 shorter events, 38.8 us)
Async XLA Ops:
  0.7 1.0 copy-start
  2.5 0.7 copy-start.2
  57.6 1.6 collective-permute-start
  58.5 1.8 collective-permute-start.1
  59.2 9.2 %collective-permute-start.4 = (f32[64,1024]{1,0:T(8,128)S(1)}, f32[64,1024]{1,0:T(8,128)S(1)}, u32[]{:S(2)}, u32[]{:S(2)}) collective-permute-start(f32[64,1024]{1,0:T(8,128)S(1)} %add.25.a), channel_id=1, source_target_pairs={{0,2},{2,0},{1,3},{3,1},{4,6},{6,4},{5,7},{7,5},{8,10},{10,8},{9,1... | collective-permute-start | bytes 786440 | tf_op jit(solution)/shard_map/ppermute | solution.py:224
  60.4 12.9 %collective-permute-start.2 = (f32[64,1024]{1,0:T(8,128)S(1)}, f32[64,1024]{1,0:T(8,128)S(1)}, u32[]{:S(2)}, u32[]{:S(2)}) collective-permute-start(f32[64,1024]{1,0:T(8,128)S(1)} %add.26.a), channel_id=1, source_target_pairs={{0,2},{2,0},{1,3},{3,1},{4,6},{6,4},{5,7},{7,5},{8,10},{10,8},{9,1... | collective-permute-start | bytes 786440 | tf_op jit(solution)/shard_map/ppermute | solution.py:224
  68.5 4.9 %collective-permute-start.5 = (f32[64,1024]{1,0:T(8,128)S(1)}, f32[64,1024]{1,0:T(8,128)S(1)}, u32[]{:S(2)}, u32[]{:S(2)}) collective-permute-start(f32[64,1024]{1,0:T(8,128)S(1)} %add.28.mine.refs_0_), channel_id=1, source_target_pairs={{0,1},{1,0},{2,3},{3,2},{4,5},{5,4},{6,7},{7,6},{8,9},{9,8},{10,11... | collective-permute-start | bytes 786440 | tf_op jit(solution)/shard_map/ppermute | solution.py:224
  73.3 1.8 collective-permute-start.3
  115.9 1.6 collective-permute-start.6
  116.9 1.8 collective-permute-start.7
  117.6 9.2 %collective-permute-start.10 = (f32[64,1024]{1,0:T(8,128)S(1)}, f32[64,1024]{1,0:T(8,128)S(1)}, u32[]{:S(2)}, u32[]{:S(2)}) collective-permute-start(f32[64,1024]{1,0:T(8,128)S(1)} %add.29.a), channel_id=1, source_target_pairs={{0,2},{2,0},{1,3},{3,1},{4,6},{6,4},{5,7},{7,5},{8,10},{10,8},{9,1... | collective-permute-start | bytes 786440 | tf_op jit(solution)/shard_map/ppermute | solution.py:224
  118.7 12.9 %collective-permute-start.8 = (f32[64,1024]{1,0:T(8,128)S(1)}, f32[64,1024]{1,0:T(8,128)S(1)}, u32[]{:S(2)}, u32[]{:S(2)}) collective-permute-start(f32[64,1024]{1,0:T(8,128)S(1)} %add.30.a), channel_id=1, source_target_pairs={{0,2},{2,0},{1,3},{3,1},{4,6},{6,4},{5,7},{7,5},{8,10},{10,8},{9,1... | collective-permute-start | bytes 786440 | tf_op jit(solution)/shard_map/ppermute | solution.py:224
  126.9 4.9 %collective-permute-start.11 = (f32[64,1024]{1,0:T(8,128)S(1)}, f32[64,1024]{1,0:T(8,128)S(1)}, u32[]{:S(2)}, u32[]{:S(2)}) collective-permute-start(f32[64,1024]{1,0:T(8,128)S(1)} %add.32.mine.refs_2_), channel_id=1, source_target_pairs={{0,1},{1,0},{2,3},{3,2},{4,5},{5,4},{6,7},{7,6},{8,9},{9,8},{10,11... | collective-permute-start | bytes 786440 | tf_op jit(solution)/shard_map/ppermute | solution.py:224
  131.7 1.8 collective-permute-start.9
  174.3 1.7 collective-permute-start.12
  175.2 2.0 collective-permute-start.13
  176.1 9.3 %collective-permute-start.16 = (f32[64,1024]{1,0:T(8,128)S(1)}, f32[64,1024]{1,0:T(8,128)S(1)}, u32[]{:S(2)}, u32[]{:S(2)}) collective-permute-start(f32[64,1024]{1,0:T(8,128)S(1)} %add.33.a), channel_id=1, source_target_pairs={{0,2},{2,0},{1,3},{3,1},{4,6},{6,4},{5,7},{7,5},{8,10},{10,8},{9,1... | collective-permute-start | bytes 786440 | tf_op jit(solution)/shard_map/ppermute | solution.py:224
  177.2 12.8 %collective-permute-start.14 = (f32[64,1024]{1,0:T(8,128)S(1)}, f32[64,1024]{1,0:T(8,128)S(1)}, u32[]{:S(2)}, u32[]{:S(2)}) collective-permute-start(f32[64,1024]{1,0:T(8,128)S(1)} %add.34.a), channel_id=1, source_target_pairs={{0,2},{2,0},{1,3},{3,1},{4,6},{6,4},{5,7},{7,5},{8,10},{10,8},{9,1... | collective-permute-start | bytes 786440 | tf_op jit(solution)/shard_map/ppermute | solution.py:224
  185.4 4.8 %collective-permute-start.17 = (f32[64,1024]{1,0:T(8,128)S(1)}, f32[64,1024]{1,0:T(8,128)S(1)}, u32[]{:S(2)}, u32[]{:S(2)}) collective-permute-start(f32[64,1024]{1,0:T(8,128)S(1)} %add.36.mine.refs_4_), channel_id=1, source_target_pairs={{0,1},{1,0},{2,3},{3,2},{4,5},{5,4},{6,7},{7,6},{8,9},{9,8},{10,11... | collective-permute-start | bytes 786440 | tf_op jit(solution)/shard_map/ppermute | solution.py:224
  190.1 1.8 collective-permute-start.15
  232.7 1.6 collective-permute-start.18
  233.6 1.7 collective-permute-start.19
  235.5 8.7 %collective-permute-start.20 = (f32[64,1024]{1,0:T(8,128)S(1)}, f32[64,1024]{1,0:T(8,128)S(1)}, u32[]{:S(2)}, u32[]{:S(2)}) collective-permute-start(f32[64,1024]{1,0:T(8,128)S(1)} %broadcast_select_fusion), channel_id=1, source_target_pairs={{0,2},{2,0},{1,3},{3,1},{4,6},{6,4},{5,7},{7,5},{8,10},{10,8},{9,1... | collective-permute-start | bytes 786440 | tf_op jit(solution)/shard_map/ppermute | solution.py:224
  244.5 1.2 collective-permute-start.21
  (1 other events, 0.7 us)

commit v3 on v2

--- a/solution.py
+++ b/solution.py
@@ -19,6 +19,7 @@
 OWN = WIDTH // 4
 PEERS = 16
 EACH = 5
+LIVE, CORE, LOW = 2 * MAXB, 2 * MAXB + 1, 2 * MAXB + 2
 PANEL = 8
 START_MIB = 40
 BATCHES = 8
@@ -102,7 +103,7 @@
     return work[:, K:] * lax.rsqrt(diagonal)
 
 
-def start_kernel(row_blocks, col_blocks, live, turn, tiles, basis, dense, packed, stock, first, sems, first_sem):
+def start_kernel(numbers, tiles, basis, dense, packed, stock, first, sems, first_sem):
     get_basis = pltpu.make_async_copy(basis, first, first_sem)
     get_basis.start()
     copies = []
@@ -110,14 +111,14 @@
         span = pl.ds(n * BATCH, BATCH)
         copies.append(pltpu.make_async_copy(tiles.at[span], stock.at[span], sems.at[n]))
         copies[-1].start()
-    core, count = turn[0], live[0]
+    core, count = numbers[CORE], numbers[LIVE]
 
     def window(s):
-        col = col_blocks[s]
+        col = numbers[MAXB + s]
         quarter = col // (CB // 4)
         position = (((quarter % 2) ^ core) * 2 + quarter // 2) * (CB // 4) + col % (CB // 4)
         return (
-            pl.ds(pl.multiple_of(row_blocks[s] * TILE, TILE), TILE),
+            pl.ds(pl.multiple_of(numbers[s] * TILE, TILE), TILE),
             pl.ds(pl.multiple_of(position * TILE, TILE), TILE),
         )
 
@@ -146,7 +147,8 @@
     return image[:K] + image[K:], grams[0] + grams[1]
 
 
-def forward_kernel(mine, other, dense, image, gram):
+def forward_kernel(mine, upper, lower, dense, image, gram):
+    other = jnp.concatenate([upper[...], lower[...]], axis=0)
     image[...], gram[...] = gathered(0, mine, other, dense)
 
 
@@ -199,6 +201,13 @@
     out[...] = a[...] + b[...]
 
 
+def add_parts_kernel(a, b, out, upper, lower):
+    total = a[...] + b[...]
+    out[...] = total
+    upper[...] = total[: K // 2]
+    lower[...] = total[K // 2 :]
+
+
 def share_kernel(parts, out):
     total = parts[0]
     for n in range(1, parts.shape[0]):
@@ -207,16 +216,18 @@
         out[n] = total
 
 
-def finish_kernel(turn, gram, *refs):
-    halves, last_half, inverses, out = refs[: 2 * ITERS - 2], refs[2 * ITERS - 2], refs[2 * ITERS - 1 : -1], refs[-1]
+def settle_kernel(numbers, inverse, half, half_last, out):
+    taken = jnp.where(numbers[LOW] == 0, half[...], half_last[...])
+    out[...] = jnp.dot(inverse[...], taken, precision=lax.Precision.HIGHEST, preferred_element_type=f32)
+
+
+def finish_kernel(gram, own, *refs):
+    settled, out = refs[:-1], refs[-1]
     whole = jnp.concatenate([gram[:, :K], gram[:, K:]], axis=0)
     last = inverse_factor(whole * (1.0 / CELLS))
-    for i in range(ITERS):
-        if i < ITERS - 1:
-            found, taken = inverses[i][...], jnp.where(turn[1] == 0, halves[2 * i][...], halves[2 * i + 1][...])
-        else:
-            found, taken = last, last_half[...]
-        out[i] = jnp.dot(found, taken, precision=lax.Precision.HIGHEST, preferred_element_type=f32)
+    for i, ready in enumerate(settled):
+        out[i] = ready[...]
+    out[ITERS - 1] = jnp.dot(last, own[...], precision=lax.Precision.HIGHEST, preferred_element_type=f32)
 
 
 def shifted(x, axis, by):
@@ -261,7 +272,8 @@
 
 def local(sens_tiles, start_basis, row_blocks, col_blocks, live_counts):
     core, low = lax.axis_index("c"), lax.axis_index("l")
-    turn = jnp.stack([core, low]).astype(jnp.int32)
+    places = [row_blocks.reshape(MAXB), col_blocks.reshape(MAXB), live_counts.reshape(1), core.reshape(1), low.reshape(1)]
+    numbers = jnp.concatenate([p.astype(jnp.int32) for p in places])
     packed_shape = ((PEERS, EACH * 8, TILE), f32)
     chunk, square, kept_shape = ((K, OWN), f32), ((K, K), f32), ((K, HEIGHT), bf16)
     work = 2 * K * HEIGHT * HALF
@@ -269,9 +281,9 @@
         start_kernel,
         "start",
         START_MIB,
-        [SMEM, SMEM, SMEM, SMEM, HBM, HBM],
+        [SMEM, HBM, HBM],
         [((HEIGHT, WIDTH), bf16), packed_shape],
-        [row_blocks.reshape(MAXB), col_blocks.reshape(MAXB), live_counts.reshape(1), turn, sens_tiles, start_basis],
+        [numbers, sens_tiles, start_basis],
         2 * work,
         [
             pltpu.VMEM(sens_tiles.shape, bf16),
@@ -280,7 +292,7 @@
             pltpu.SemaphoreType.DMA,
         ],
     )
-    halves, inverses = [], []
+    halves, settled = None, []
     for iteration in range(ITERS):
         packed = summed_over_blk(packed)
         if iteration == 0:
@@ -289,7 +301,9 @@
             mine, other, kept, inverse = call(
                 backward_kernel, "backward", 8, [VMEM, VMEM], [chunk, chunk, kept_shape, square], [packed, dense], work
             )
-            inverses.append(inverse)
+            settled.append(
+                call(settle_kernel, "settle", 4, [SMEM] + [VMEM] * 3, [chunk], [numbers, inverse, *halves], 6 * 2 * K * K * OWN)
+            )
         moving = shifted(other, "c", 1)
         mine_last, other_last = call(backward_last_kernel, "backward_last", 8, [VMEM, VMEM], [chunk, chunk], [kept, dense], work)
         mine = added(mine, moving)
@@ -303,10 +317,18 @@
         mine_last = added(mine_last, shifted(other_last, "c", 1))
         moving_last = shifted(mine_last, "l", 1)
         mine, mine_last = lax.optimization_barrier((mine, mine_last))
-        mine = added(mine, moving)
+        part = ((K // 2, OWN), f32)
+        mine, upper, lower = call(add_parts_kernel, "add_parts", 4, [VMEM, VMEM], [chunk, part, part], [mine, moving])
         image, gram = call(
-            forward_kernel, "forward", 12, [VMEM, VMEM, VMEM], [chunk, square], [mine, shifted(mine, "c", 1), dense], 2 * work
+            forward_kernel,
+            "forward",
+            12,
+            [VMEM] * 4,
+            [chunk, square],
+            [mine, shifted(upper, "c", 1), shifted(lower, "c", 1), dense],
+            2 * work,
         )
+        mine_last, image, gram = lax.optimization_barrier((mine_last, image, gram))
         mine_last = added(mine_last, moving_last)
         packed = call(
             forward_last_kernel,
@@ -317,16 +339,11 @@
             [mine_last, shifted(mine_last, "c", 1), dense, image, gram],
             2 * work,
         )
-        halves += [mine, mine_last]
+        halves = mine, mine_last
     gram = call(gram_kernel, "gram", 50, [VMEM], [((K // 2, 2 * K), f32)], [own])
     gram = summed_by_all(summed_by_all(gram + shifted(gram, "c", 1), PLANE), ("h", "l"))
     return call(
-        finish_kernel,
-        "finish",
-        50,
-        [SMEM] + [VMEM] * (3 * ITERS - 1),
-        [((ITERS, K, OWN), f32)],
-        [turn, gram, *halves, own, *inverses],
+        finish_kernel, "finish", 50, [VMEM] * (ITERS + 1), [((ITERS, K, OWN), f32)], [gram, own, *settled]
     )
 
 

time: 274 us -> 287 us (1.047); the launches traced: 274 us -> 283 us
  starting transfers between devices: 11.3 us -> 25.5 us
  blocking collectives: 174 us -> 161 us
  waiting for transfers between devices: 45 us -> 49.9 us
    all_to_all x2 -> x1, blocking collectives: 23.4 us -> 11.9 us  [summed_by_all(): lax.all_to_all(jnp.broadcast_to(x[None], (count, *x.shape)), axes, 0, 0,...]
    ppermute x22 -> x25, starting transfers between devices: 11.3 us -> 22.1 us  [shifted(): return lax.ppermute(x, axis, [(i, (i + by) % count) for i in range(count)])]
    all_to_all x0 -> x1, waiting for transfers between devices: none -> 6.13 us  [summed_by_all(): lax.all_to_all(jnp.broadcast_to(x[None], (count, *x.shape)), axes, 0, 0,...]
    all_to_all x0 -> x1, starting transfers between devices: none -> 3.37 us  [summed_by_all(): lax.all_to_all(jnp.broadcast_to(x[None], (count, *x.shape)), axes, 0, 0,...]
    pallas_call x39 -> x42, Pallas kernels: 40.1 us -> 42.3 us  [call(): pl.pallas_call(kernel, out_shape=shapes, in_specs=ins, out_specs=(VMEM,)...]
    ppermute x22 -> x25, waiting for transfers between devices: 45 us -> 43.7 us  [shifted(): return lax.ppermute(x, axis, [(i, (i + by) % count) for i in range(count)])]
  transfers between devices with their start and end apart: 22 -> 26, of which waited for: 12 -> 24; matrix products, arithmetic and copies ran while one was open for 0% -> 0% of each run, Pallas kernels for 3% -> 4%
where the time goes in v3:
time: 287 us; the launch traced here: 283 us
  blocking collectives  161 us (56%)
  waiting for transfers between devices  49.9 us (17%)
  Pallas kernels  42.3 us (15%)
  starting transfers between devices  25.5 us (9%)
    all_to_all x4, blocking collectives, summed_over_blk(): shares = lax.all_to_all(packed, PLANE, 0, 0, tiled=True)  53 us
    all_to_all x4, blocking collectives, summed_over_blk(): shares = lax.all_to_all(shared(shares, 4), 'h', 0, 0, tiled=True)  48.7 us
    all_to_all x4, blocking collectives, summed_over_blk(): return lax.all_to_all(shared(shares, PEERS), PLANE, 0, 0, tiled=True)  47.8 us
    ppermute x25, waiting for transfers between devices, shifted(): return lax.ppermute(x, axis, [(i, (i + by) % count) for i in range(count)])  43.7 us
    pallas_call x42, Pallas kernels, call(): pl.pallas_call(kernel, out_shape=shapes, in_specs=ins, out_specs=(VMEM,)...  42.3 us
    ppermute x25, starting transfers between devices, shifted(): return lax.ppermute(x, axis, [(i, (i + by) % count) for i in range(count)])  22.1 us
    all_to_all x1, blocking collectives, summed_by_all(): lax.all_to_all(jnp.broadcast_to(x[None], (count, *x.shape)), axes, 0, 0,...  11.9 us
    all_to_all x1, waiting for transfers between devices, summed_by_all(): lax.all_to_all(jnp.broadcast_to(x[None], (count, *x.shape)), axes, 0, 0,...  6.13 us
  transfers between devices with their start and end apart: 26, of which 24 were waited for; matrix products, arithmetic and copies ran while one was open for 0% of the time, Pallas kernels for 4%

profile of v3, /device:TPU:2, one launch (start us, length us, event | category | flops | bytes accessed | tf_op | source)
XLA Modules:
  0.0 283.0 jit_solution(739460945762647922)
XLA Ops:
  2.5 9.8 %start.1 = (bf16[1024,4096]{1,0:T(8,128)(2,1)S(1)}, f32[16,40,128]{2,1,0:T(8,128)S(1)}) custom-call(s32[515]{0:T(1024)S(1)} %concatenate.3.numbers, bf16[256,128,128]{2,1,0:T(8,128)(2,1)} %tiles.1, bf16[64,4096]{1,0:T(8,128)(2,1)S(1)} %copy-done), custom_call_target="tpu_custom_call" | custom-call | flops 536870912 | bytes 17631244 | tf_op jit(solution)/shard_map/start/pallas_call | solution.py:246
  12.3 15.3 %all_to_all.70.parts = f32[16,40,128]{2,1,0:T(8,128)S(1)} all-to-all(f32[16,40,128]{2,1,0:T(8,128)S(1)} %get-tuple-element.60), channel_id=1, replica_groups=mesh['y'=4,'x'=4,'h'=4,'l'=2,'c'=2] {'y','x'}, dimensions={0} | all-to-all | bytes 655360 | tf_op jit(solution)/shard_map/all_to_all | solution.py:268
  27.6 16.6 %all_to_all.71.parts = f32[4,40,128]{2,1,0:T(8,128)S(1)} all-to-all(f32[4,40,128]{2,1,0:T(8,128)S(1)} %share.8), channel_id=1, replica_groups=mesh['y'=4,'x'=4,'h'=4,'l'=2,'c'=2] {'h'}, dimensions={0} | all-to-all | bytes 163840 | tf_op jit(solution)/shard_map/all_to_all | solution.py:269
  44.2 11.9 %all_to_all.72.packed = f32[16,40,128]{2,1,0:T(8,128)S(1)} all-to-all(f32[16,40,128]{2,1,0:T(8,128)S(1)} %share.9), channel_id=1, replica_groups=mesh['y'=4,'x'=4,'h'=4,'l'=2,'c'=2] {'y','x'}, dimensions={0} | all-to-all | bytes 655360 | tf_op jit(solution)/shard_map/all_to_all | solution.py:270
  60.8 7.0 %collective-permute-done.2.b = f32[64,1024]{1,0:T(8,128)S(1)} collective-permute-done((f32[64,1024]{1,0:T(8,128)S(1)}, f32[64,1024]{1,0:T(8,128)S(1)}, u32[]{:S(2)}, u32[]{:S(2)}) %collective-permute-start.2) | collective-permute-done | bytes 262176 | tf_op jit(solution)/shard_map/ppermute | solution.py:235
  76.0 12.6 %all_to_all.73.parts = f32[16,40,128]{2,1,0:T(8,128)S(1)} all-to-all(f32[16,40,128]{2,1,0:T(8,128)S(1)} %forward_last.3), channel_id=1, replica_groups=mesh['y'=4,'x'=4,'h'=4,'l'=2,'c'=2] {'y','x'}, dimensions={0} | all-to-all | bytes 655360 | tf_op jit(solution)/shard_map/all_to_all | solution.py:268
  88.6 10.7 %all_to_all.74.parts = f32[4,40,128]{2,1,0:T(8,128)S(1)} all-to-all(f32[4,40,128]{2,1,0:T(8,128)S(1)} %share.10), channel_id=1, replica_groups=mesh['y'=4,'x'=4,'h'=4,'l'=2,'c'=2] {'h'}, dimensions={0} | all-to-all | bytes 163840 | tf_op jit(solution)/shard_map/all_to_all | solution.py:269
  99.3 12.1 %all_to_all.75.packed = f32[16,40,128]{2,1,0:T(8,128)S(1)} all-to-all(f32[16,40,128]{2,1,0:T(8,128)S(1)} %share.11), channel_id=1, replica_groups=mesh['y'=4,'x'=4,'h'=4,'l'=2,'c'=2] {'y','x'}, dimensions={0} | all-to-all | bytes 655360 | tf_op jit(solution)/shard_map/all_to_all | solution.py:270
  111.5 3.6 %backward.5 = (f32[64,1024]{1,0:T(8,128)S(1)}, f32[64,1024]{1,0:T(8,128)S(1)}, bf16[64,1024]{1,0:T(8,128)(2,1)S(1)}, f32[64,64]{1,0:T(8,128)S(1)}) custom-call(f32[16,40,128]{2,1,0:T(8,128)S(1)} %all_to_all.75.packed, bf16[1024,4096]{1,0:T(8,128)(2,1)S(1)} %get-tuple-element.61.dense), custom_call_target="tpu_custom_call" | custom-call | flops 268435456 | bytes 9388032 | tf_op jit(solution)/shard_map/backward/pallas_call | solution.py:246
  119.0 7.0 %collective-permute-done.9.b = f32[64,1024]{1,0:T(8,128)S(1)} collective-permute-done((f32[64,1024]{1,0:T(8,128)S(1)}, f32[64,1024]{1,0:T(8,128)S(1)}, u32[]{:S(2)}, u32[]{:S(2)}) %collective-permute-start.9) | collective-permute-done | bytes 262176 | tf_op jit(solution)/shard_map/ppermute | solution.py:235
  134.1 12.6 %all_to_all.76.parts = f32[16,40,128]{2,1,0:T(8,128)S(1)} all-to-all(f32[16,40,128]{2,1,0:T(8,128)S(1)} %forward_last.4), channel_id=1, replica_groups=mesh['y'=4,'x'=4,'h'=4,'l'=2,'c'=2] {'y','x'}, dimensions={0} | all-to-all | bytes 655360 | tf_op jit(solution)/shard_map/all_to_all | solution.py:268
  146.7 10.7 %all_to_all.77.parts = f32[4,40,128]{2,1,0:T(8,128)S(1)} all-to-all(f32[4,40,128]{2,1,0:T(8,128)S(1)} %share.12), channel_id=1, replica_groups=mesh['y'=4,'x'=4,'h'=4,'l'=2,'c'=2] {'h'}, dimensions={0} | all-to-all | bytes 163840 | tf_op jit(solution)/shard_map/all_to_all | solution.py:269
  157.4 11.9 %all_to_all.78.packed = f32[16,40,128]{2,1,0:T(8,128)S(1)} all-to-all(f32[16,40,128]{2,1,0:T(8,128)S(1)} %share.13), channel_id=1, replica_groups=mesh['y'=4,'x'=4,'h'=4,'l'=2,'c'=2] {'y','x'}, dimensions={0} | all-to-all | bytes 655360 | tf_op jit(solution)/shard_map/all_to_all | solution.py:270
  169.3 3.6 %backward.6 = (f32[64,1024]{1,0:T(8,128)S(1)}, f32[64,1024]{1,0:T(8,128)S(1)}, bf16[64,1024]{1,0:T(8,128)(2,1)S(1)}, f32[64,64]{1,0:T(8,128)S(1)}) custom-call(f32[16,40,128]{2,1,0:T(8,128)S(1)} %all_to_all.78.packed, bf16[1024,4096]{1,0:T(8,128)(2,1)S(1)} %get-tuple-element.61.dense), custom_call_target="tpu_custom_call" | custom-call | flops 268435456 | bytes 9388032 | tf_op jit(solution)/shard_map/backward/pallas_call | solution.py:246
  172.9 10.2 %collective-permute-start.14 = (f32[64,1024]{1,0:T(8,128)S(1)}, f32[64,1024]{1,0:T(8,128)S(1)}, u32[]{:S(2)}, u32[]{:S(2)}) collective-permute-start(f32[64,1024]{1,0:T(8,128)S(1)} %get-tuple-element.93), channel_id=1, source_target_pairs={{0,1},{1,0},{2,3},{3,2},{4,5},{5,4},{6,7},{7,6},{8,9},{9,8},{10,11... | collective-permute-start | bytes 786440 | tf_op jit(solution)/shard_map/ppermute | solution.py:235
  186.9 7.0 %collective-permute-done.16.b = f32[64,1024]{1,0:T(8,128)S(1)} collective-permute-done((f32[64,1024]{1,0:T(8,128)S(1)}, f32[64,1024]{1,0:T(8,128)S(1)}, u32[]{:S(2)}, u32[]{:S(2)}) %collective-permute-start.16) | collective-permute-done | bytes 262176 | tf_op jit(solution)/shard_map/ppermute | solution.py:235
  202.1 12.6 %all_to_all.79.parts = f32[16,40,128]{2,1,0:T(8,128)S(1)} all-to-all(f32[16,40,128]{2,1,0:T(8,128)S(1)} %forward_last.5), channel_id=1, replica_groups=mesh['y'=4,'x'=4,'h'=4,'l'=2,'c'=2] {'y','x'}, dimensions={0} | all-to-all | bytes 655360 | tf_op jit(solution)/shard_map/all_to_all | solution.py:268
  214.7 10.7 %all_to_all.80.parts = f32[4,40,128]{2,1,0:T(8,128)S(1)} all-to-all(f32[4,40,128]{2,1,0:T(8,128)S(1)} %share.14), channel_id=1, replica_groups=mesh['y'=4,'x'=4,'h'=4,'l'=2,'c'=2] {'h'}, dimensions={0} | all-to-all | bytes 163840 | tf_op jit(solution)/shard_map/all_to_all | solution.py:269
  225.4 11.9 %all_to_all.81.packed = f32[16,40,128]{2,1,0:T(8,128)S(1)} all-to-all(f32[16,40,128]{2,1,0:T(8,128)S(1)} %share.15), channel_id=1, replica_groups=mesh['y'=4,'x'=4,'h'=4,'l'=2,'c'=2] {'y','x'}, dimensions={0} | all-to-all | bytes 655360 | tf_op jit(solution)/shard_map/all_to_all | solution.py:270
  237.3 3.6 %backward.7 = (f32[64,1024]{1,0:T(8,128)S(1)}, f32[64,1024]{1,0:T(8,128)S(1)}, bf16[64,1024]{1,0:T(8,128)(2,1)S(1)}, f32[64,64]{1,0:T(8,128)S(1)}) custom-call(f32[16,40,128]{2,1,0:T(8,128)S(1)} %all_to_all.81.packed, bf16[1024,4096]{1,0:T(8,128)(2,1)S(1)} %get-tuple-element.61.dense), custom_call_target="tpu_custom_call" | custom-call | flops 268435456 | bytes 9388032 | tf_op jit(solution)/shard_map/backward/pallas_call | solution.py:246
  244.4 7.9 %collective-permute-done.23 = f32[64,1024]{1,0:T(8,128)S(1)} collective-permute-done((f32[64,1024]{1,0:T(8,128)S(1)}, f32[64,1024]{1,0:T(8,128)S(1)}, u32[]{:S(2)}, u32[]{:S(2)}) %collective-permute-start.23) | collective-permute-done | bytes 262176 | tf_op jit(solution)/shard_map/ppermute | solution.py:235
  254.0 11.9 %all_to_all.82 = f32[16,32,128]{2,1,0:T(8,128)S(1)} all-to-all(f32[16,32,128]{2,1,0:T(8,128)S(1)} %broadcast_in_dim.4), channel_id=1, replica_groups=mesh['y'=4,'x'=4,'h'=4,'l'=2,'c'=2] {'y','x'}, dimensions={0} | all-to-all | bytes 524288 | tf_op jit(solution)/shard_map/all_to_all | solution.py:240
  272.8 6.1 %all-to-all-done.13 = f32[8,32,128]{2,1,0:T(8,128)S(1)} async-done(((f32[8,32,128]{2,1,0:T(8,128)}), f32[8,32,128]{2,1,0:T(8,128)S(1)}, u32[]{:S(2)}, u32[]{:S(2)}) %all-to-all-start.13) | async-done | bytes 131104 | tf_op jit(solution)/shard_map/all_to_all | solution.py:240
  279.0 3.8 %finish.1 = f32[4,64,1024]{2,1,0:T(8,128)} custom-call(f32[32,128]{1,0:T(8,128)S(1)} %reduce_sum.19.gram, f32[64,1024]{1,0:T(8,128)S(1)} %select_add_fusion.own, f32[64,1024]{1,0:T(8,128)S(1)} %settle.3.refs_0_, f32[64,1024]{1,0:T(8,128)S(1)} %settle.4.refs_1_, f32[64,1024]{1,0:T(8,128)S(1)} %settle.5.refs_2_), custom_call_target="tpu_custom_call" | custom-call | bytes 2113536 | tf_op jit(solution)/shard_map/finish/pallas_call | solution.py:246
  (93 shorter events, 50.8 us)
Async XLA Ops:
  57.0 1.6 collective-permute-start
  57.9 1.8 collective-permute-start.1
  58.6 9.2 %collective-permute-start.2 = (f32[64,1024]{1,0:T(8,128)S(1)}, f32[64,1024]{1,0:T(8,128)S(1)}, u32[]{:S(2)}, u32[]{:S(2)}) collective-permute-start(f32[64,1024]{1,0:T(8,128)S(1)} %add.20.a), channel_id=1, source_target_pairs={{0,2},{2,0},{1,3},{3,1},{4,6},{6,4},{5,7},{7,5},{8,10},{10,8},{9,1... | collective-permute-start | bytes 786440 | tf_op jit(solution)/shard_map/ppermute | solution.py:235
  59.7 12.9 %collective-permute-start.5 = (f32[64,1024]{1,0:T(8,128)S(1)}, f32[64,1024]{1,0:T(8,128)S(1)}, u32[]{:S(2)}, u32[]{:S(2)}) collective-permute-start(f32[64,1024]{1,0:T(8,128)S(1)} %add.21.a), channel_id=1, source_target_pairs={{0,2},{2,0},{1,3},{3,1},{4,6},{6,4},{5,7},{7,5},{8,10},{10,8},{9,1... | collective-permute-start | bytes 786440 | tf_op jit(solution)/shard_map/ppermute | solution.py:235
  67.9 1.4 collective-permute-start.3
  68.0 1.5 collective-permute-start.4
  72.7 1.6 collective-permute-start.6
  115.1 1.6 collective-permute-start.7
  116.0 1.7 collective-permute-start.8
  116.7 9.2 %collective-permute-start.9 = (f32[64,1024]{1,0:T(8,128)S(1)}, f32[64,1024]{1,0:T(8,128)S(1)}, u32[]{:S(2)}, u32[]{:S(2)}) collective-permute-start(f32[64,1024]{1,0:T(8,128)S(1)} %add.23.a), channel_id=1, source_target_pairs={{0,2},{2,0},{1,3},{3,1},{4,6},{6,4},{5,7},{7,5},{8,10},{10,8},{9,1... | collective-permute-start | bytes 786440 | tf_op jit(solution)/shard_map/ppermute | solution.py:235
  117.8 13.0 %collective-permute-start.12 = (f32[64,1024]{1,0:T(8,128)S(1)}, f32[64,1024]{1,0:T(8,128)S(1)}, u32[]{:S(2)}, u32[]{:S(2)}) collective-permute-start(f32[64,1024]{1,0:T(8,128)S(1)} %add.24.a), channel_id=1, source_target_pairs={{0,2},{2,0},{1,3},{3,1},{4,6},{6,4},{5,7},{7,5},{8,10},{10,8},{9,1... | collective-permute-start | bytes 786440 | tf_op jit(solution)/shard_map/ppermute | solution.py:235
  126.0 1.4 collective-permute-start.10
  126.1 1.5 collective-permute-start.11
  130.8 1.6 collective-permute-start.13
  172.9 11.7 %collective-permute-start.14 = (f32[64,1024]{1,0:T(8,128)S(1)}, f32[64,1024]{1,0:T(8,128)S(1)}, u32[]{:S(2)}, u32[]{:S(2)}) collective-permute-start(f32[64,1024]{1,0:T(8,128)S(1)} %get-tuple-element.93), channel_id=1, source_target_pairs={{0,1},{1,0},{2,3},{3,2},{4,5},{5,4},{6,7},{7,6},{8,9},{9,8},{10,11... | collective-permute-start | bytes 786440 | tf_op jit(solution)/shard_map/ppermute | solution.py:235
  184.0 1.7 collective-permute-start.15
  184.7 9.2 %collective-permute-start.16 = (f32[64,1024]{1,0:T(8,128)S(1)}, f32[64,1024]{1,0:T(8,128)S(1)}, u32[]{:S(2)}, u32[]{:S(2)}) collective-permute-start(f32[64,1024]{1,0:T(8,128)S(1)} %add.26.a), channel_id=1, source_target_pairs={{0,2},{2,0},{1,3},{3,1},{4,6},{6,4},{5,7},{7,5},{8,10},{10,8},{9,1... | collective-permute-start | bytes 786440 | tf_op jit(solution)/shard_map/ppermute | solution.py:235
  185.7 13.0 %collective-permute-start.19 = (f32[64,1024]{1,0:T(8,128)S(1)}, f32[64,1024]{1,0:T(8,128)S(1)}, u32[]{:S(2)}, u32[]{:S(2)}) collective-permute-start(f32[64,1024]{1,0:T(8,128)S(1)} %add.27.a), channel_id=1, source_target_pairs={{0,2},{2,0},{1,3},{3,1},{4,6},{6,4},{5,7},{7,5},{8,10},{10,8},{9,1... | collective-permute-start | bytes 786440 | tf_op jit(solution)/shard_map/ppermute | solution.py:235
  194.1 1.5 collective-permute-start.18
  198.8 1.6 collective-permute-start.20
  240.9 1.6 collective-permute-start.21
  241.8 1.7 collective-permute-start.22
  243.6 8.7 %collective-permute-start.23 = (f32[64,1024]{1,0:T(8,128)S(1)}, f32[64,1024]{1,0:T(8,128)S(1)}, u32[]{:S(2)}, u32[]{:S(2)}) collective-permute-start(f32[64,1024]{1,0:T(8,128)S(1)} %broadcast_select_fusion), channel_id=1, source_target_pairs={{0,2},{2,0},{1,3},{3,1},{4,6},{6,4},{5,7},{7,5},{8,10},{10,8},{9,1... | collective-permute-start | bytes 786440 | tf_op jit(solution)/shard_map/ppermute | solution.py:235
  266.6 12.4 %all-to-all-start.13 = ((f32[8,32,128]{2,1,0:T(8,128)}), f32[8,32,128]{2,1,0:T(8,128)S(1)}, u32[]{:S(2)}, u32[]{:S(2)}) async-start(f32[8,32,128]{2,1,0:T(8,128)} %broadcast_in_dim.5), calls=%async_computation.13 | async-start | bytes 262144 | tf_op jit(solution)/shard_map/all_to_all | solution.py:240
  (3 other events, 3.7 us)

commit v4 on v3

--- a/solution.py
+++ b/solution.py
@@ -138,24 +138,28 @@
     write_packed(packed, image, None)
 
 
-def gathered(chunk, mine, other, dense):
-    image, grams = 0.0, []
-    for p, half in ((chunk, mine), (2 + chunk, other)):
-        parts = two_parts(half[...])
-        grams.append(gram_of(parts))
-        image = image + dot_rows(parts, dense[:, p * OWN : (p + 1) * OWN])
-    return image[:K] + image[K:], grams[0] + grams[1]
+def gathered(p, half, dense):
+    parts = two_parts(half)
+    image = dot_rows(parts, dense[:, p * OWN : (p + 1) * OWN])
+    return image[:K] + image[K:], gram_of(parts)
 
 
 def forward_kernel(mine, upper, lower, dense, image, gram):
-    other = jnp.concatenate([upper[...], lower[...]], axis=0)
-    image[...], gram[...] = gathered(0, mine, other, dense)
-
-
-def forward_last_kernel(mine, other, dense, image_before, gram_before, packed):
-    image, gram = gathered(1, mine, other, dense)
-    gram = gram_before[...] + gram
-    write_packed(packed, image_before[...] + image, jnp.concatenate([gram, gram], axis=1))
+    image_mine, gram_mine = gathered(0, mine[...], dense)
+    image_other, gram_other = gathered(2, jnp.concatenate([upper[...], lower[...]], axis=0), dense)
+    image[...] = image_mine + image_other
+    gram[...] = gram_mine + gram_other
+
+
+def forward_mine_kernel(mine, dense, image_before, image, gram):
+    found, gram[...] = gathered(1, mine[...], dense)
+    image[...] = image_before[...] + found
+
+
+def forward_last_kernel(other, dense, image_before, gram_before, gram_mine, packed):
+    found, gram_other = gathered(3, other[...], dense)
+    gram = gram_before[...] + (gram_mine[...] + gram_other)
+    write_packed(packed, image_before[...] + found, jnp.concatenate([gram, gram], axis=1))
 
 
 def gram_kernel(own, out):
@@ -310,6 +314,7 @@
         if iteration == ITERS - 1:
             mine_last = added(mine_last, shifted(other_last, "c", 1))
             own = jnp.where(low == 0, mine, mine_last)
+            own, *settled = lax.optimization_barrier((own, *settled))
             sent = jnp.where(low == 0, mine_last, mine)
             own = own + shifted(sent, "l", 1)
             break
@@ -317,6 +322,7 @@
         mine_last = added(mine_last, shifted(other_last, "c", 1))
         moving_last = shifted(mine_last, "l", 1)
         mine, mine_last = lax.optimization_barrier((mine, mine_last))
+        mine, *settled = lax.optimization_barrier((mine, *settled))
         part = ((K // 2, OWN), f32)
         mine, upper, lower = call(add_parts_kernel, "add_parts", 4, [VMEM, VMEM], [chunk, part, part], [mine, moving])
         image, gram = call(
@@ -330,14 +336,18 @@
         )
         mine_last, image, gram = lax.optimization_barrier((mine_last, image, gram))
         mine_last = added(mine_last, moving_last)
+        other_last = shifted(mine_last, "c", 1)
+        image, gram_mine = call(
+            forward_mine_kernel, "forward_mine", 12, [VMEM] * 3, [chunk, square], [mine_last, dense, image], work
+        )
         packed = call(
             forward_last_kernel,
             "forward_last",
             12,
             [VMEM] * 5,
             [packed_shape],
-            [mine_last, shifted(mine_last, "c", 1), dense, image, gram],
-            2 * work,
+            [other_last, dense, image, gram, gram_mine],
+            work,
         )
         halves = mine, mine_last
     gram = call(gram_kernel, "gram", 50, [VMEM], [((K // 2, 2 * K), f32)], [own])

time: 287 us -> 283 us (0.986)
  blocking collectives: 161 us -> 173 us
  waiting for transfers between devices: 49.9 us -> 37.9 us
  starting transfers between devices: 25.5 us -> 22 us
    all_to_all x1 -> x2, blocking collectives: 11.9 us -> 23.4 us  [summed_by_all(): lax.all_to_all(jnp.broadcast_to(x[None], (count, *x.shape)), axes, 0, 0,...]
    all_to_all x1 -> x0, waiting for transfers between devices: 6.13 us -> none  [summed_by_all(): lax.all_to_all(jnp.broadcast_to(x[None], (count, *x.shape)), axes, 0, 0,...]
    ppermute x25, waiting for transfers between devices: 43.7 us -> 37.9 us  [shifted(): return lax.ppermute(x, axis, [(i, (i + by) % count) for i in range(count)])]
    all_to_all x1 -> x0, starting transfers between devices: 3.37 us -> none  [summed_by_all(): lax.all_to_all(jnp.broadcast_to(x[None], (count, *x.shape)), axes, 0, 0,...]
    pallas_call x42 -> x45, Pallas kernels: 42.3 us -> 43.2 us  [call(): pl.pallas_call(kernel, out_shape=shapes, in_specs=ins, out_specs=(VMEM,)...]
  transfers between devices with their start and end apart: 26 -> 25, of which waited for: 24 -> 23; matrix products, arithmetic and copies ran while one was open for 0% -> 0% of each run, Pallas kernels for 4% -> 5%
where the time goes in v4:
time: 283 us; the launch traced here: 279 us
  blocking collectives  173 us (61%)
  Pallas kernels  43.2 us (15%)
  waiting for transfers between devices  37.9 us (13%)
  starting transfers between devices  22 us (8%)
    all_to_all x4, blocking collectives, summed_over_blk(): shares = lax.all_to_all(packed, PLANE, 0, 0, tiled=True)  53 us
    all_to_all x4, blocking collectives, summed_over_blk(): shares = lax.all_to_all(shared(shares, 4), 'h', 0, 0, tiled=True)  48.7 us
    all_to_all x4, blocking collectives, summed_over_blk(): return lax.all_to_all(shared(shares, PEERS), PLANE, 0, 0, tiled=True)  47.8 us
    pallas_call x45, Pallas kernels, call(): pl.pallas_call(kernel, out_shape=shapes, in_specs=ins, out_specs=(VMEM,)...  43.2 us
    ppermute x25, waiting for transfers between devices, shifted(): return lax.ppermute(x, axis, [(i, (i + by) % count) for i in range(count)])  37.9 us
    all_to_all x2, blocking collectives, summed_by_all(): lax.all_to_all(jnp.broadcast_to(x[None], (count, *x.shape)), axes, 0, 0,...  23.4 us
    ppermute x25, starting transfers between devices, shifted(): return lax.ppermute(x, axis, [(i, (i + by) % count) for i in range(count)])  22 us
  transfers between devices with their start and end apart: 25, of which 23 were waited for; matrix products, arithmetic and copies ran while one was open for 0% of the time, Pallas kernels for 5%

profile of v4, /device:TPU:2, one launch (start us, length us, event | category | flops | bytes accessed | tf_op | source)
XLA Modules:
  0.0 279.2 jit_solution(8181225339191729909)
XLA Ops:
  2.5 9.8 %start.1 = (bf16[1024,4096]{1,0:T(8,128)(2,1)S(1)}, f32[16,40,128]{2,1,0:T(8,128)S(1)}) custom-call(s32[515]{0:T(1024)S(1)} %concatenate.3.numbers, bf16[256,128,128]{2,1,0:T(8,128)(2,1)} %tiles.1, bf16[64,4096]{1,0:T(8,128)(2,1)S(1)} %copy-done), custom_call_target="tpu_custom_call" | custom-call | flops 536870912 | bytes 17631244 | tf_op jit(solution)/shard_map/start/pallas_call | solution.py:250
  12.3 15.3 %all_to_all.70.parts = f32[16,40,128]{2,1,0:T(8,128)S(1)} all-to-all(f32[16,40,128]{2,1,0:T(8,128)S(1)} %get-tuple-element.75), channel_id=1, replica_groups=mesh['y'=4,'x'=4,'h'=4,'l'=2,'c'=2] {'y','x'}, dimensions={0} | all-to-all | bytes 655360 | tf_op jit(solution)/shard_map/all_to_all | solution.py:272
  27.6 16.6 %all_to_all.71.parts = f32[4,40,128]{2,1,0:T(8,128)S(1)} all-to-all(f32[4,40,128]{2,1,0:T(8,128)S(1)} %share.8), channel_id=1, replica_groups=mesh['y'=4,'x'=4,'h'=4,'l'=2,'c'=2] {'h'}, dimensions={0} | all-to-all | bytes 163840 | tf_op jit(solution)/shard_map/all_to_all | solution.py:273
  44.2 11.9 %all_to_all.72.packed = f32[16,40,128]{2,1,0:T(8,128)S(1)} all-to-all(f32[16,40,128]{2,1,0:T(8,128)S(1)} %share.9), channel_id=1, replica_groups=mesh['y'=4,'x'=4,'h'=4,'l'=2,'c'=2] {'y','x'}, dimensions={0} | all-to-all | bytes 655360 | tf_op jit(solution)/shard_map/all_to_all | solution.py:274
  60.8 7.0 %collective-permute-done.2.b = f32[64,1024]{1,0:T(8,128)S(1)} collective-permute-done((f32[64,1024]{1,0:T(8,128)S(1)}, f32[64,1024]{1,0:T(8,128)S(1)}, u32[]{:S(2)}, u32[]{:S(2)}) %collective-permute-start.2) | collective-permute-done | bytes 262176 | tf_op jit(solution)/shard_map/ppermute | solution.py:239
  75.3 12.6 %all_to_all.73.parts = f32[16,40,128]{2,1,0:T(8,128)S(1)} all-to-all(f32[16,40,128]{2,1,0:T(8,128)S(1)} %forward_last.3), channel_id=1, replica_groups=mesh['y'=4,'x'=4,'h'=4,'l'=2,'c'=2] {'y','x'}, dimensions={0} | all-to-all | bytes 655360 | tf_op jit(solution)/shard_map/all_to_all | solution.py:272
  87.9 10.7 %all_to_all.74.parts = f32[4,40,128]{2,1,0:T(8,128)S(1)} all-to-all(f32[4,40,128]{2,1,0:T(8,128)S(1)} %share.10), channel_id=1, replica_groups=mesh['y'=4,'x'=4,'h'=4,'l'=2,'c'=2] {'h'}, dimensions={0} | all-to-all | bytes 163840 | tf_op jit(solution)/shard_map/all_to_all | solution.py:273
  98.7 12.1 %all_to_all.75.packed = f32[16,40,128]{2,1,0:T(8,128)S(1)} all-to-all(f32[16,40,128]{2,1,0:T(8,128)S(1)} %share.11), channel_id=1, replica_groups=mesh['y'=4,'x'=4,'h'=4,'l'=2,'c'=2] {'y','x'}, dimensions={0} | all-to-all | bytes 655360 | tf_op jit(solution)/shard_map/all_to_all | solution.py:274
  110.8 3.6 %backward.5 = (f32[64,1024]{1,0:T(8,128)S(1)}, f32[64,1024]{1,0:T(8,128)S(1)}, bf16[64,1024]{1,0:T(8,128)(2,1)S(1)}, f32[64,64]{1,0:T(8,128)S(1)}) custom-call(f32[16,40,128]{2,1,0:T(8,128)S(1)} %all_to_all.75.packed, bf16[1024,4096]{1,0:T(8,128)(2,1)S(1)} %get-tuple-element.76.dense), custom_call_target="tpu_custom_call" | custom-call | flops 268435456 | bytes 9388032 | tf_op jit(solution)/shard_map/backward/pallas_call | solution.py:250
  119.2 6.0 %collective-permute-done.9.b = f32[64,1024]{1,0:T(8,128)S(1)} collective-permute-done((f32[64,1024]{1,0:T(8,128)S(1)}, f32[64,1024]{1,0:T(8,128)S(1)}, u32[]{:S(2)}, u32[]{:S(2)}) %collective-permute-start.9) | collective-permute-done | bytes 262176 | tf_op jit(solution)/shard_map/ppermute | solution.py:239
  132.8 12.6 %all_to_all.76.parts = f32[16,40,128]{2,1,0:T(8,128)S(1)} all-to-all(f32[16,40,128]{2,1,0:T(8,128)S(1)} %forward_last.4), channel_id=1, replica_groups=mesh['y'=4,'x'=4,'h'=4,'l'=2,'c'=2] {'y','x'}, dimensions={0} | all-to-all | bytes 655360 | tf_op jit(solution)/shard_map/all_to_all | solution.py:272
  145.4 10.7 %all_to_all.77.parts = f32[4,40,128]{2,1,0:T(8,128)S(1)} all-to-all(f32[4,40,128]{2,1,0:T(8,128)S(1)} %share.12), channel_id=1, replica_groups=mesh['y'=4,'x'=4,'h'=4,'l'=2,'c'=2] {'h'}, dimensions={0} | all-to-all | bytes 163840 | tf_op jit(solution)/shard_map/all_to_all | solution.py:273
  156.1 11.9 %all_to_all.78.packed = f32[16,40,128]{2,1,0:T(8,128)S(1)} all-to-all(f32[16,40,128]{2,1,0:T(8,128)S(1)} %share.13), channel_id=1, replica_groups=mesh['y'=4,'x'=4,'h'=4,'l'=2,'c'=2] {'y','x'}, dimensions={0} | all-to-all | bytes 655360 | tf_op jit(solution)/shard_map/all_to_all | solution.py:274
  168.0 3.6 %backward.6 = (f32[64,1024]{1,0:T(8,128)S(1)}, f32[64,1024]{1,0:T(8,128)S(1)}, bf16[64,1024]{1,0:T(8,128)(2,1)S(1)}, f32[64,64]{1,0:T(8,128)S(1)}) custom-call(f32[16,40,128]{2,1,0:T(8,128)S(1)} %all_to_all.78.packed, bf16[1024,4096]{1,0:T(8,128)(2,1)S(1)} %get-tuple-element.76.dense), custom_call_target="tpu_custom_call" | custom-call | flops 268435456 | bytes 9388032 | tf_op jit(solution)/shard_map/backward/pallas_call | solution.py:250
  171.6 10.0 %collective-permute-start.14 = (f32[64,1024]{1,0:T(8,128)S(1)}, f32[64,1024]{1,0:T(8,128)S(1)}, u32[]{:S(2)}, u32[]{:S(2)}) collective-permute-start(f32[64,1024]{1,0:T(8,128)S(1)} %get-tuple-element.114), channel_id=1, source_target_pairs={{0,1},{1,0},{2,3},{3,2},{4,5},{5,4},{6,7},{7,6},{8,9},{9,8},{10,11... | collective-permute-start | bytes 786440 | tf_op jit(solution)/shard_map/ppermute | solution.py:239
  186.3 6.0 %collective-permute-done.16.b = f32[64,1024]{1,0:T(8,128)S(1)} collective-permute-done((f32[64,1024]{1,0:T(8,128)S(1)}, f32[64,1024]{1,0:T(8,128)S(1)}, u32[]{:S(2)}, u32[]{:S(2)}) %collective-permute-start.16) | collective-permute-done | bytes 262176 | tf_op jit(solution)/shard_map/ppermute | solution.py:239
  199.8 12.6 %all_to_all.79.parts = f32[16,40,128]{2,1,0:T(8,128)S(1)} all-to-all(f32[16,40,128]{2,1,0:T(8,128)S(1)} %forward_last.5), channel_id=1, replica_groups=mesh['y'=4,'x'=4,'h'=4,'l'=2,'c'=2] {'y','x'}, dimensions={0} | all-to-all | bytes 655360 | tf_op jit(solution)/shard_map/all_to_all | solution.py:272
  212.4 10.7 %all_to_all.80.parts = f32[4,40,128]{2,1,0:T(8,128)S(1)} all-to-all(f32[4,40,128]{2,1,0:T(8,128)S(1)} %share.14), channel_id=1, replica_groups=mesh['y'=4,'x'=4,'h'=4,'l'=2,'c'=2] {'h'}, dimensions={0} | all-to-all | bytes 163840 | tf_op jit(solution)/shard_map/all_to_all | solution.py:273
  223.2 11.9 %all_to_all.81.packed = f32[16,40,128]{2,1,0:T(8,128)S(1)} all-to-all(f32[16,40,128]{2,1,0:T(8,128)S(1)} %share.15), channel_id=1, replica_groups=mesh['y'=4,'x'=4,'h'=4,'l'=2,'c'=2] {'y','x'}, dimensions={0} | all-to-all | bytes 655360 | tf_op jit(solution)/shard_map/all_to_all | solution.py:274
  235.1 3.6 %backward.7 = (f32[64,1024]{1,0:T(8,128)S(1)}, f32[64,1024]{1,0:T(8,128)S(1)}, bf16[64,1024]{1,0:T(8,128)(2,1)S(1)}, f32[64,64]{1,0:T(8,128)S(1)}) custom-call(f32[16,40,128]{2,1,0:T(8,128)S(1)} %all_to_all.81.packed, bf16[1024,4096]{1,0:T(8,128)(2,1)S(1)} %get-tuple-element.76.dense), custom_call_target="tpu_custom_call" | custom-call | flops 268435456 | bytes 9388032 | tf_op jit(solution)/shard_map/backward/pallas_call | solution.py:250
  243.2 6.9 %collective-permute-done.23 = f32[64,1024]{1,0:T(8,128)S(1)} collective-permute-done((f32[64,1024]{1,0:T(8,128)S(1)}, f32[64,1024]{1,0:T(8,128)S(1)}, u32[]{:S(2)}, u32[]{:S(2)}) %collective-permute-start.23) | collective-permute-done | bytes 262176 | tf_op jit(solution)/shard_map/ppermute | solution.py:239
  251.7 11.9 %all_to_all.82 = f32[16,32,128]{2,1,0:T(8,128)S(1)} all-to-all(f32[16,32,128]{2,1,0:T(8,128)S(1)} %broadcast_in_dim.4), channel_id=1, replica_groups=mesh['y'=4,'x'=4,'h'=4,'l'=2,'c'=2] {'y','x'}, dimensions={0} | all-to-all | bytes 524288 | tf_op jit(solution)/shard_map/all_to_all | solution.py:244
  263.7 11.5 %all_to_all.83 = f32[8,32,128]{2,1,0:T(8,128)S(1)} all-to-all(f32[8,32,128]{2,1,0:T(8,128)S(1)} %broadcast_in_dim.5), channel_id=1, replica_groups=mesh['y'=4,'x'=4,'h'=4,'l'=2,'c'=2] {'h','l'}, dimensions={0} | all-to-all | bytes 262144 | tf_op jit(solution)/shard_map/all_to_all | solution.py:244
  275.2 3.8 %finish.1 = f32[4,64,1024]{2,1,0:T(8,128)} custom-call(f32[32,128]{1,0:T(8,128)S(1)} %reduce_sum.19.gram, f32[64,1024]{1,0:T(8,128)S(1)} %add.17.own, f32[64,1024]{1,0:T(8,128)S(1)} %settle.3.refs_0_, f32[64,1024]{1,0:T(8,128)S(1)} %settle.4.refs_1_, f32[64,1024]{1,0:T(8,128)S(1)} %settle.5.refs_2_), custom_call_target="tpu_custom_call" | custom-call | bytes 2113536 | tf_op jit(solution)/shard_map/finish/pallas_call | solution.py:250
  (95 shorter events, 44.8 us)
Async XLA Ops:
  57.0 1.6 collective-permute-start
  57.9 1.8 collective-permute-start.1
  58.6 9.2 %collective-permute-start.2 = (f32[64,1024]{1,0:T(8,128)S(1)}, f32[64,1024]{1,0:T(8,128)S(1)}, u32[]{:S(2)}, u32[]{:S(2)}) collective-permute-start(f32[64,1024]{1,0:T(8,128)S(1)} %add.19.a), channel_id=1, source_target_pairs={{0,2},{2,0},{1,3},{3,1},{4,6},{6,4},{5,7},{7,5},{8,10},{10,8},{9,1... | collective-permute-start | bytes 786440 | tf_op jit(solution)/shard_map/ppermute | solution.py:239
  59.8 12.9 %collective-permute-start.5 = (f32[64,1024]{1,0:T(8,128)S(1)}, f32[64,1024]{1,0:T(8,128)S(1)}, u32[]{:S(2)}, u32[]{:S(2)}) collective-permute-start(f32[64,1024]{1,0:T(8,128)S(1)} %add.20.a), channel_id=1, source_target_pairs={{0,2},{2,0},{1,3},{3,1},{4,6},{6,4},{5,7},{7,5},{8,10},{10,8},{9,1... | collective-permute-start | bytes 786440 | tf_op jit(solution)/shard_map/ppermute | solution.py:239
  67.9 1.4 collective-permute-start.3
  68.0 1.5 collective-permute-start.4
  72.7 1.6 collective-permute-start.6
  114.4 1.6 collective-permute-start.7
  115.3 1.7 collective-permute-start.8
  116.1 9.2 %collective-permute-start.9 = (f32[64,1024]{1,0:T(8,128)S(1)}, f32[64,1024]{1,0:T(8,128)S(1)}, u32[]{:S(2)}, u32[]{:S(2)}) collective-permute-start(f32[64,1024]{1,0:T(8,128)S(1)} %add.22.a), channel_id=1, source_target_pairs={{0,2},{2,0},{1,3},{3,1},{4,6},{6,4},{5,7},{7,5},{8,10},{10,8},{9,1... | collective-permute-start | bytes 786440 | tf_op jit(solution)/shard_map/ppermute | solution.py:239
  117.1 13.0 %collective-permute-start.12 = (f32[64,1024]{1,0:T(8,128)S(1)}, f32[64,1024]{1,0:T(8,128)S(1)}, u32[]{:S(2)}, u32[]{:S(2)}) collective-permute-start(f32[64,1024]{1,0:T(8,128)S(1)} %add.23.a), channel_id=1, source_target_pairs={{0,2},{2,0},{1,3},{3,1},{4,6},{6,4},{5,7},{7,5},{8,10},{10,8},{9,1... | collective-permute-start | bytes 786440 | tf_op jit(solution)/shard_map/ppermute | solution.py:239
  125.3 1.4 collective-permute-start.10
  125.4 1.5 collective-permute-start.11
  130.1 1.6 collective-permute-start.13
  171.6 11.5 %collective-permute-start.14 = (f32[64,1024]{1,0:T(8,128)S(1)}, f32[64,1024]{1,0:T(8,128)S(1)}, u32[]{:S(2)}, u32[]{:S(2)}) collective-permute-start(f32[64,1024]{1,0:T(8,128)S(1)} %get-tuple-element.114), channel_id=1, source_target_pairs={{0,1},{1,0},{2,3},{3,2},{4,5},{5,4},{6,7},{7,6},{8,9},{9,8},{10,11... | collective-permute-start | bytes 786440 | tf_op jit(solution)/shard_map/ppermute | solution.py:239
  182.4 1.7 collective-permute-start.15
  183.1 9.2 %collective-permute-start.16 = (f32[64,1024]{1,0:T(8,128)S(1)}, f32[64,1024]{1,0:T(8,128)S(1)}, u32[]{:S(2)}, u32[]{:S(2)}) collective-permute-start(f32[64,1024]{1,0:T(8,128)S(1)} %add.25.a), channel_id=1, source_target_pairs={{0,2},{2,0},{1,3},{3,1},{4,6},{6,4},{5,7},{7,5},{8,10},{10,8},{9,1... | collective-permute-start | bytes 786440 | tf_op jit(solution)/shard_map/ppermute | solution.py:239
  184.2 13.0 %collective-permute-start.19 = (f32[64,1024]{1,0:T(8,128)S(1)}, f32[64,1024]{1,0:T(8,128)S(1)}, u32[]{:S(2)}, u32[]{:S(2)}) collective-permute-start(f32[64,1024]{1,0:T(8,128)S(1)} %add.26.a), channel_id=1, source_target_pairs={{0,2},{2,0},{1,3},{3,1},{4,6},{6,4},{5,7},{7,5},{8,10},{10,8},{9,1... | collective-permute-start | bytes 786440 | tf_op jit(solution)/shard_map/ppermute | solution.py:239
  192.4 1.4 collective-permute-start.17
  192.5 1.5 collective-permute-start.18
  197.2 1.6 collective-permute-start.20
  238.6 1.6 collective-permute-start.21
  239.6 1.7 collective-permute-start.22
  241.4 8.7 %collective-permute-start.23 = (f32[64,1024]{1,0:T(8,128)S(1)}, f32[64,1024]{1,0:T(8,128)S(1)}, u32[]{:S(2)}, u32[]{:S(2)}) collective-permute-start(f32[64,1024]{1,0:T(8,128)S(1)} %get-tuple-element.145), channel_id=1, source_target_pairs={{0,2},{2,0},{1,3},{3,1},{4,6},{6,4},{5,7},{7,5},{8,10},{10,8},{9,1... | collective-permute-start | bytes 786440 | tf_op jit(solution)/shard_map/ppermute | solution.py:239
  (2 other events, 2.3 us)

commit v5 on v4

--- a/solution.py
+++ b/solution.py
@@ -19,7 +19,6 @@
 OWN = WIDTH // 4
 PEERS = 16
 EACH = 5
-LIVE, CORE, LOW = 2 * MAXB, 2 * MAXB + 1, 2 * MAXB + 2
 PANEL = 8
 START_MIB = 40
 BATCHES = 8
@@ -103,7 +102,7 @@
     return work[:, K:] * lax.rsqrt(diagonal)
 
 
-def start_kernel(numbers, tiles, basis, dense, packed, stock, first, sems, first_sem):
+def start_kernel(row_blocks, col_blocks, live, turn, tiles, basis, dense, packed, stock, first, sems, first_sem):
     get_basis = pltpu.make_async_copy(basis, first, first_sem)
     get_basis.start()
     copies = []
@@ -111,14 +110,14 @@
         span = pl.ds(n * BATCH, BATCH)
         copies.append(pltpu.make_async_copy(tiles.at[span], stock.at[span], sems.at[n]))
         copies[-1].start()
-    core, count = numbers[CORE], numbers[LIVE]
+    core, count = turn[0], live[0]
 
     def window(s):
-        col = numbers[MAXB + s]
+        col = col_blocks[s]
         quarter = col // (CB // 4)
         position = (((quarter % 2) ^ core) * 2 + quarter // 2) * (CB // 4) + col % (CB // 4)
         return (
-            pl.ds(pl.multiple_of(numbers[s] * TILE, TILE), TILE),
+            pl.ds(pl.multiple_of(row_blocks[s] * TILE, TILE), TILE),
             pl.ds(pl.multiple_of(position * TILE, TILE), TILE),
         )
 
@@ -220,8 +219,8 @@
         out[n] = total
 
 
-def settle_kernel(numbers, inverse, half, half_last, out):
-    taken = jnp.where(numbers[LOW] == 0, half[...], half_last[...])
+def settle_kernel(turn, inverse, half, half_last, out):
+    taken = jnp.where(turn[1] == 0, half[...], half_last[...])
     out[...] = jnp.dot(inverse[...], taken, precision=lax.Precision.HIGHEST, preferred_element_type=f32)
 
 
@@ -276,8 +275,7 @@
 
 def local(sens_tiles, start_basis, row_blocks, col_blocks, live_counts):
     core, low = lax.axis_index("c"), lax.axis_index("l")
-    places = [row_blocks.reshape(MAXB), col_blocks.reshape(MAXB), live_counts.reshape(1), core.reshape(1), low.reshape(1)]
-    numbers = jnp.concatenate([p.astype(jnp.int32) for p in places])
+    turn = jnp.stack([core, low]).astype(jnp.int32)
     packed_shape = ((PEERS, EACH * 8, TILE), f32)
     chunk, square, kept_shape = ((K, OWN), f32), ((K, K), f32), ((K, HEIGHT), bf16)
     work = 2 * K * HEIGHT * HALF
@@ -285,9 +283,9 @@
         start_kernel,
         "start",
         START_MIB,
-        [SMEM, HBM, HBM],
+        [SMEM, SMEM, SMEM, SMEM, HBM, HBM],
         [((HEIGHT, WIDTH), bf16), packed_shape],
-        [numbers, sens_tiles, start_basis],
+        [row_blocks.reshape(MAXB), col_blocks.reshape(MAXB), live_counts.reshape(1), turn, sens_tiles, start_basis],
         2 * work,
         [
             pltpu.VMEM(sens_tiles.shape, bf16),
@@ -306,7 +304,7 @@
                 backward_kernel, "backward", 8, [VMEM, VMEM], [chunk, chunk, kept_shape, square], [packed, dense], work
             )
             settled.append(
-                call(settle_kernel, "settle", 4, [SMEM] + [VMEM] * 3, [chunk], [numbers, inverse, *halves], 6 * 2 * K * K * OWN)
+                call(settle_kernel, "settle", 4, [SMEM] + [VMEM] * 3, [chunk], [turn, inverse, *halves], 6 * 2 * K * K * OWN)
             )
         moving = shifted(other, "c", 1)
         mine_last, other_last = call(backward_last_kernel, "backward_last", 8, [VMEM, VMEM], [chunk, chunk], [kept, dense], work)

time: 283 us -> 283 us (level)
  no operation moved by 1% of the time
where the time goes in v5:
time: 283 us; the launch traced here: 280 us
  blocking collectives  173 us (61%)
  Pallas kernels  43.1 us (15%)
  waiting for transfers between devices  37.8 us (13%)
  starting transfers between devices  22.1 us (8%)
    all_to_all x4, blocking collectives, summed_over_blk(): shares = lax.all_to_all(packed, PLANE, 0, 0, tiled=True)  53 us
    all_to_all x4, blocking collectives, summed_over_blk(): shares = lax.all_to_all(shared(shares, 4), 'h', 0, 0, tiled=True)  48.7 us
    all_to_all x4, blocking collectives, summed_over_blk(): return lax.all_to_all(shared(shares, PEERS), PLANE, 0, 0, tiled=True)  47.8 us
    pallas_call x45, Pallas kernels, call(): pl.pallas_call(kernel, out_shape=shapes, in_specs=ins, out_specs=(VMEM,)...  43.1 us
    ppermute x25, waiting for transfers between devices, shifted(): return lax.ppermute(x, axis, [(i, (i + by) % count) for i in range(count)])  37.8 us
    all_to_all x2, blocking collectives, summed_by_all(): lax.all_to_all(jnp.broadcast_to(x[None], (count, *x.shape)), axes, 0, 0,...  23.4 us
    ppermute x25, starting transfers between devices, shifted(): return lax.ppermute(x, axis, [(i, (i + by) % count) for i in range(count)])  22.1 us
  transfers between devices with their start and end apart: 25, of which 23 were waited for; matrix products, arithmetic and copies ran while one was open for 0% of the time, Pallas kernels for 5%

profile of v5, /device:TPU:2, one launch (start us, length us, event | category | flops | bytes accessed | tf_op | source)
XLA Modules:
  0.0 279.8 jit_solution(10274880166522413335)
XLA Ops:
  3.1 9.7 %start.1 = (bf16[1024,4096]{1,0:T(8,128)(2,1)S(1)}, f32[16,40,128]{2,1,0:T(8,128)S(1)}) custom-call(s32[256]{0:T(256)S(1)} %bitcast.6, s32[256]{0:T(256)S(1)} %bitcast.7, s32[1]{0:T(128)} %bitcast.5.live, s32[2]{0:T(128)S(1)} %pad_add_fusion.turn, bf16[256,128,128]{2,1,0:T(8,128)(2,1)} %tiles.1, bf16[64,4096]{1,0:T(8,128)(2,1)S(1)} %copy-done), custom_call_target="tpu_custom_call" | custom-call | flops 536870912 | bytes 17631244 | tf_op jit(solution)/shard_map/start/pallas_call | solution.py:249
  12.9 15.3 %all_to_all.70.parts = f32[16,40,128]{2,1,0:T(8,128)S(1)} all-to-all(f32[16,40,128]{2,1,0:T(8,128)S(1)} %get-tuple-element.75), channel_id=1, replica_groups=mesh['y'=4,'x'=4,'h'=4,'l'=2,'c'=2] {'y','x'}, dimensions={0} | all-to-all | bytes 655360 | tf_op jit(solution)/shard_map/all_to_all | solution.py:271
  28.2 16.6 %all_to_all.71.parts = f32[4,40,128]{2,1,0:T(8,128)S(1)} all-to-all(f32[4,40,128]{2,1,0:T(8,128)S(1)} %share.8), channel_id=1, replica_groups=mesh['y'=4,'x'=4,'h'=4,'l'=2,'c'=2] {'h'}, dimensions={0} | all-to-all | bytes 163840 | tf_op jit(solution)/shard_map/all_to_all | solution.py:272
  44.8 11.9 %all_to_all.72.packed = f32[16,40,128]{2,1,0:T(8,128)S(1)} all-to-all(f32[16,40,128]{2,1,0:T(8,128)S(1)} %share.9), channel_id=1, replica_groups=mesh['y'=4,'x'=4,'h'=4,'l'=2,'c'=2] {'y','x'}, dimensions={0} | all-to-all | bytes 655360 | tf_op jit(solution)/shard_map/all_to_all | solution.py:273
  61.4 7.0 %collective-permute-done.2.b = f32[64,1024]{1,0:T(8,128)S(1)} collective-permute-done((f32[64,1024]{1,0:T(8,128)S(1)}, f32[64,1024]{1,0:T(8,128)S(1)}, u32[]{:S(2)}, u32[]{:S(2)}) %collective-permute-start.2) | collective-permute-done | bytes 262176 | tf_op jit(solution)/shard_map/ppermute | solution.py:238
  75.9 12.6 %all_to_all.73.parts = f32[16,40,128]{2,1,0:T(8,128)S(1)} all-to-all(f32[16,40,128]{2,1,0:T(8,128)S(1)} %forward_last.3), channel_id=1, replica_groups=mesh['y'=4,'x'=4,'h'=4,'l'=2,'c'=2] {'y','x'}, dimensions={0} | all-to-all | bytes 655360 | tf_op jit(solution)/shard_map/all_to_all | solution.py:271
  88.5 10.7 %all_to_all.74.parts = f32[4,40,128]{2,1,0:T(8,128)S(1)} all-to-all(f32[4,40,128]{2,1,0:T(8,128)S(1)} %share.10), channel_id=1, replica_groups=mesh['y'=4,'x'=4,'h'=4,'l'=2,'c'=2] {'h'}, dimensions={0} | all-to-all | bytes 163840 | tf_op jit(solution)/shard_map/all_to_all | solution.py:272
  99.3 12.1 %all_to_all.75.packed = f32[16,40,128]{2,1,0:T(8,128)S(1)} all-to-all(f32[16,40,128]{2,1,0:T(8,128)S(1)} %share.11), channel_id=1, replica_groups=mesh['y'=4,'x'=4,'h'=4,'l'=2,'c'=2] {'y','x'}, dimensions={0} | all-to-all | bytes 655360 | tf_op jit(solution)/shard_map/all_to_all | solution.py:273
  111.4 3.6 %backward.5 = (f32[64,1024]{1,0:T(8,128)S(1)}, f32[64,1024]{1,0:T(8,128)S(1)}, bf16[64,1024]{1,0:T(8,128)(2,1)S(1)}, f32[64,64]{1,0:T(8,128)S(1)}) custom-call(f32[16,40,128]{2,1,0:T(8,128)S(1)} %all_to_all.75.packed, bf16[1024,4096]{1,0:T(8,128)(2,1)S(1)} %get-tuple-element.76.dense), custom_call_target="tpu_custom_call" | custom-call | flops 268435456 | bytes 9388032 | tf_op jit(solution)/shard_map/backward/pallas_call | solution.py:249
  119.8 6.1 %collective-permute-done.9.b = f32[64,1024]{1,0:T(8,128)S(1)} collective-permute-done((f32[64,1024]{1,0:T(8,128)S(1)}, f32[64,1024]{1,0:T(8,128)S(1)}, u32[]{:S(2)}, u32[]{:S(2)}) %collective-permute-start.9) | collective-permute-done | bytes 262176 | tf_op jit(solution)/shard_map/ppermute | solution.py:238
  133.4 12.6 %all_to_all.76.parts = f32[16,40,128]{2,1,0:T(8,128)S(1)} all-to-all(f32[16,40,128]{2,1,0:T(8,128)S(1)} %forward_last.4), channel_id=1, replica_groups=mesh['y'=4,'x'=4,'h'=4,'l'=2,'c'=2] {'y','x'}, dimensions={0} | all-to-all | bytes 655360 | tf_op jit(solution)/shard_map/all_to_all | solution.py:271
  146.0 10.7 %all_to_all.77.parts = f32[4,40,128]{2,1,0:T(8,128)S(1)} all-to-all(f32[4,40,128]{2,1,0:T(8,128)S(1)} %share.12), channel_id=1, replica_groups=mesh['y'=4,'x'=4,'h'=4,'l'=2,'c'=2] {'h'}, dimensions={0} | all-to-all | bytes 163840 | tf_op jit(solution)/shard_map/all_to_all | solution.py:272
  156.7 11.9 %all_to_all.78.packed = f32[16,40,128]{2,1,0:T(8,128)S(1)} all-to-all(f32[16,40,128]{2,1,0:T(8,128)S(1)} %share.13), channel_id=1, replica_groups=mesh['y'=4,'x'=4,'h'=4,'l'=2,'c'=2] {'y','x'}, dimensions={0} | all-to-all | bytes 655360 | tf_op jit(solution)/shard_map/all_to_all | solution.py:273
  168.6 3.6 %backward.6 = (f32[64,1024]{1,0:T(8,128)S(1)}, f32[64,1024]{1,0:T(8,128)S(1)}, bf16[64,1024]{1,0:T(8,128)(2,1)S(1)}, f32[64,64]{1,0:T(8,128)S(1)}) custom-call(f32[16,40,128]{2,1,0:T(8,128)S(1)} %all_to_all.78.packed, bf16[1024,4096]{1,0:T(8,128)(2,1)S(1)} %get-tuple-element.76.dense), custom_call_target="tpu_custom_call" | custom-call | flops 268435456 | bytes 9388032 | tf_op jit(solution)/shard_map/backward/pallas_call | solution.py:249
  172.2 10.0 %collective-permute-start.14 = (f32[64,1024]{1,0:T(8,128)S(1)}, f32[64,1024]{1,0:T(8,128)S(1)}, u32[]{:S(2)}, u32[]{:S(2)}) collective-permute-start(f32[64,1024]{1,0:T(8,128)S(1)} %get-tuple-element.114), channel_id=1, source_target_pairs={{0,1},{1,0},{2,3},{3,2},{4,5},{5,4},{6,7},{7,6},{8,9},{9,8},{10,11... | collective-permute-start | bytes 786440 | tf_op jit(solution)/shard_map/ppermute | solution.py:238
  186.9 6.1 %collective-permute-done.16.b = f32[64,1024]{1,0:T(8,128)S(1)} collective-permute-done((f32[64,1024]{1,0:T(8,128)S(1)}, f32[64,1024]{1,0:T(8,128)S(1)}, u32[]{:S(2)}, u32[]{:S(2)}) %collective-permute-start.16) | collective-permute-done | bytes 262176 | tf_op jit(solution)/shard_map/ppermute | solution.py:238
  200.4 12.6 %all_to_all.79.parts = f32[16,40,128]{2,1,0:T(8,128)S(1)} all-to-all(f32[16,40,128]{2,1,0:T(8,128)S(1)} %forward_last.5), channel_id=1, replica_groups=mesh['y'=4,'x'=4,'h'=4,'l'=2,'c'=2] {'y','x'}, dimensions={0} | all-to-all | bytes 655360 | tf_op jit(solution)/shard_map/all_to_all | solution.py:271
  213.0 10.7 %all_to_all.80.parts = f32[4,40,128]{2,1,0:T(8,128)S(1)} all-to-all(f32[4,40,128]{2,1,0:T(8,128)S(1)} %share.14), channel_id=1, replica_groups=mesh['y'=4,'x'=4,'h'=4,'l'=2,'c'=2] {'h'}, dimensions={0} | all-to-all | bytes 163840 | tf_op jit(solution)/shard_map/all_to_all | solution.py:272
  223.8 11.9 %all_to_all.81.packed = f32[16,40,128]{2,1,0:T(8,128)S(1)} all-to-all(f32[16,40,128]{2,1,0:T(8,128)S(1)} %share.15), channel_id=1, replica_groups=mesh['y'=4,'x'=4,'h'=4,'l'=2,'c'=2] {'y','x'}, dimensions={0} | all-to-all | bytes 655360 | tf_op jit(solution)/shard_map/all_to_all | solution.py:273
  235.7 3.6 %backward.7 = (f32[64,1024]{1,0:T(8,128)S(1)}, f32[64,1024]{1,0:T(8,128)S(1)}, bf16[64,1024]{1,0:T(8,128)(2,1)S(1)}, f32[64,64]{1,0:T(8,128)S(1)}) custom-call(f32[16,40,128]{2,1,0:T(8,128)S(1)} %all_to_all.81.packed, bf16[1024,4096]{1,0:T(8,128)(2,1)S(1)} %get-tuple-element.76.dense), custom_call_target="tpu_custom_call" | custom-call | flops 268435456 | bytes 9388032 | tf_op jit(solution)/shard_map/backward/pallas_call | solution.py:249
  243.9 6.7 %collective-permute-done.23 = f32[64,1024]{1,0:T(8,128)S(1)} collective-permute-done((f32[64,1024]{1,0:T(8,128)S(1)}, f32[64,1024]{1,0:T(8,128)S(1)}, u32[]{:S(2)}, u32[]{:S(2)}) %collective-permute-start.23) | collective-permute-done | bytes 262176 | tf_op jit(solution)/shard_map/ppermute | solution.py:238
  252.3 11.9 %all_to_all.82 = f32[16,32,128]{2,1,0:T(8,128)S(1)} all-to-all(f32[16,32,128]{2,1,0:T(8,128)S(1)} %broadcast_in_dim.4), channel_id=1, replica_groups=mesh['y'=4,'x'=4,'h'=4,'l'=2,'c'=2] {'y','x'}, dimensions={0} | all-to-all | bytes 524288 | tf_op jit(solution)/shard_map/all_to_all | solution.py:243
  264.3 11.5 %all_to_all.83 = f32[8,32,128]{2,1,0:T(8,128)S(1)} all-to-all(f32[8,32,128]{2,1,0:T(8,128)S(1)} %broadcast_in_dim.5), channel_id=1, replica_groups=mesh['y'=4,'x'=4,'h'=4,'l'=2,'c'=2] {'h','l'}, dimensions={0} | all-to-all | bytes 262144 | tf_op jit(solution)/shard_map/all_to_all | solution.py:243
  275.8 3.8 %finish.1 = f32[4,64,1024]{2,1,0:T(8,128)} custom-call(f32[32,128]{1,0:T(8,128)S(1)} %reduce_sum.19.gram, f32[64,1024]{1,0:T(8,128)S(1)} %add.17.own, f32[64,1024]{1,0:T(8,128)S(1)} %settle.3.refs_0_, f32[64,1024]{1,0:T(8,128)S(1)} %settle.4.refs_1_, f32[64,1024]{1,0:T(8,128)S(1)} %settle.5.refs_2_), custom_call_target="tpu_custom_call" | custom-call | bytes 2113536 | tf_op jit(solution)/shard_map/finish/pallas_call | solution.py:249
  (99 shorter events, 45.5 us)
Async XLA Ops:
  57.6 1.6 collective-permute-start
  58.5 1.8 collective-permute-start.1
  59.2 9.2 %collective-permute-start.2 = (f32[64,1024]{1,0:T(8,128)S(1)}, f32[64,1024]{1,0:T(8,128)S(1)}, u32[]{:S(2)}, u32[]{:S(2)}) collective-permute-start(f32[64,1024]{1,0:T(8,128)S(1)} %add.21.a), channel_id=1, source_target_pairs={{0,2},{2,0},{1,3},{3,1},{4,6},{6,4},{5,7},{7,5},{8,10},{10,8},{9,1... | collective-permute-start | bytes 786440 | tf_op jit(solution)/shard_map/ppermute | solution.py:238
  60.3 12.9 %collective-permute-start.5 = (f32[64,1024]{1,0:T(8,128)S(1)}, f32[64,1024]{1,0:T(8,128)S(1)}, u32[]{:S(2)}, u32[]{:S(2)}) collective-permute-start(f32[64,1024]{1,0:T(8,128)S(1)} %add.22.a), channel_id=1, source_target_pairs={{0,2},{2,0},{1,3},{3,1},{4,6},{6,4},{5,7},{7,5},{8,10},{10,8},{9,1... | collective-permute-start | bytes 786440 | tf_op jit(solution)/shard_map/ppermute | solution.py:238
  68.5 1.4 collective-permute-start.3
  68.6 1.5 collective-permute-start.4
  73.3 1.6 collective-permute-start.6
  115.0 1.6 collective-permute-start.7
  115.9 1.7 collective-permute-start.8
  116.6 9.2 %collective-permute-start.9 = (f32[64,1024]{1,0:T(8,128)S(1)}, f32[64,1024]{1,0:T(8,128)S(1)}, u32[]{:S(2)}, u32[]{:S(2)}) collective-permute-start(f32[64,1024]{1,0:T(8,128)S(1)} %add.24.a), channel_id=1, source_target_pairs={{0,2},{2,0},{1,3},{3,1},{4,6},{6,4},{5,7},{7,5},{8,10},{10,8},{9,1... | collective-permute-start | bytes 786440 | tf_op jit(solution)/shard_map/ppermute | solution.py:238
  117.7 13.0 %collective-permute-start.12 = (f32[64,1024]{1,0:T(8,128)S(1)}, f32[64,1024]{1,0:T(8,128)S(1)}, u32[]{:S(2)}, u32[]{:S(2)}) collective-permute-start(f32[64,1024]{1,0:T(8,128)S(1)} %add.25.a), channel_id=1, source_target_pairs={{0,2},{2,0},{1,3},{3,1},{4,6},{6,4},{5,7},{7,5},{8,10},{10,8},{9,1... | collective-permute-start | bytes 786440 | tf_op jit(solution)/shard_map/ppermute | solution.py:238
  125.9 1.4 collective-permute-start.10
  126.0 1.5 collective-permute-start.11
  130.7 1.6 collective-permute-start.13
  172.2 11.5 %collective-permute-start.14 = (f32[64,1024]{1,0:T(8,128)S(1)}, f32[64,1024]{1,0:T(8,128)S(1)}, u32[]{:S(2)}, u32[]{:S(2)}) collective-permute-start(f32[64,1024]{1,0:T(8,128)S(1)} %get-tuple-element.114), channel_id=1, source_target_pairs={{0,1},{1,0},{2,3},{3,2},{4,5},{5,4},{6,7},{7,6},{8,9},{9,8},{10,11... | collective-permute-start | bytes 786440 | tf_op jit(solution)/shard_map/ppermute | solution.py:238
  183.0 1.7 collective-permute-start.15
  183.7 9.2 %collective-permute-start.16 = (f32[64,1024]{1,0:T(8,128)S(1)}, f32[64,1024]{1,0:T(8,128)S(1)}, u32[]{:S(2)}, u32[]{:S(2)}) collective-permute-start(f32[64,1024]{1,0:T(8,128)S(1)} %add.27.a), channel_id=1, source_target_pairs={{0,2},{2,0},{1,3},{3,1},{4,6},{6,4},{5,7},{7,5},{8,10},{10,8},{9,1... | collective-permute-start | bytes 786440 | tf_op jit(solution)/shard_map/ppermute | solution.py:238
  184.8 13.0 %collective-permute-start.19 = (f32[64,1024]{1,0:T(8,128)S(1)}, f32[64,1024]{1,0:T(8,128)S(1)}, u32[]{:S(2)}, u32[]{:S(2)}) collective-permute-start(f32[64,1024]{1,0:T(8,128)S(1)} %add.28.a), channel_id=1, source_target_pairs={{0,2},{2,0},{1,3},{3,1},{4,6},{6,4},{5,7},{7,5},{8,10},{10,8},{9,1... | collective-permute-start | bytes 786440 | tf_op jit(solution)/shard_map/ppermute | solution.py:238
  193.0 1.4 collective-permute-start.17
  193.1 1.5 collective-permute-start.18
  197.8 1.6 collective-permute-start.20
  239.2 1.6 collective-permute-start.21
  240.2 1.7 collective-permute-start.22
  242.0 8.7 %collective-permute-start.23 = (f32[64,1024]{1,0:T(8,128)S(1)}, f32[64,1024]{1,0:T(8,128)S(1)}, u32[]{:S(2)}, u32[]{:S(2)}) collective-permute-start(f32[64,1024]{1,0:T(8,128)S(1)} %get-tuple-element.145), channel_id=1, source_target_pairs={{0,2},{2,0},{1,3},{3,1},{4,6},{6,4},{5,7},{7,5},{8,10},{10,8},{9,1... | collective-permute-start | bytes 786440 | tf_op jit(solution)/shard_map/ppermute | solution.py:238
  (4 other events, 3.6 us)

commit v6 on v5

--- a/solution.py
+++ b/solution.py
@@ -219,18 +219,16 @@
         out[n] = total
 
 
-def settle_kernel(turn, inverse, half, half_last, out):
-    taken = jnp.where(turn[1] == 0, half[...], half_last[...])
-    out[...] = jnp.dot(inverse[...], taken, precision=lax.Precision.HIGHEST, preferred_element_type=f32)
-
-
-def finish_kernel(gram, own, *refs):
-    settled, out = refs[:-1], refs[-1]
+def finish_kernel(turn, gram, *refs):
+    halves, last_half, inverses, out = refs[: 2 * ITERS - 2], refs[2 * ITERS - 2], refs[2 * ITERS - 1 : -1], refs[-1]
     whole = jnp.concatenate([gram[:, :K], gram[:, K:]], axis=0)
     last = inverse_factor(whole * (1.0 / CELLS))
-    for i, ready in enumerate(settled):
-        out[i] = ready[...]
-    out[ITERS - 1] = jnp.dot(last, own[...], precision=lax.Precision.HIGHEST, preferred_element_type=f32)
+    for i in range(ITERS):
+        if i < ITERS - 1:
+            found, taken = inverses[i][...], jnp.where(turn[1] == 0, halves[2 * i][...], halves[2 * i + 1][...])
+        else:
+            found, taken = last, last_half[...]
+        out[i] = jnp.dot(found, taken, precision=lax.Precision.HIGHEST, preferred_element_type=f32)
 
 
 def shifted(x, axis, by):
@@ -294,7 +292,7 @@
             pltpu.SemaphoreType.DMA,
         ],
     )
-    halves, settled = None, []
+    halves, inverses = [], []
     for iteration in range(ITERS):
         packed = summed_over_blk(packed)
         if iteration == 0:
@@ -303,16 +301,13 @@
             mine, other, kept, inverse = call(
                 backward_kernel, "backward", 8, [VMEM, VMEM], [chunk, chunk, kept_shape, square], [packed, dense], work
             )
-            settled.append(
-                call(settle_kernel, "settle", 4, [SMEM] + [VMEM] * 3, [chunk], [turn, inverse, *halves], 6 * 2 * K * K * OWN)
-            )
+            inverses.append(inverse)
         moving = shifted(other, "c", 1)
         mine_last, other_last = call(backward_last_kernel, "backward_last", 8, [VMEM, VMEM], [chunk, chunk], [kept, dense], work)
         mine = added(mine, moving)
         if iteration == ITERS - 1:
             mine_last = added(mine_last, shifted(other_last, "c", 1))
             own = jnp.where(low == 0, mine, mine_last)
-            own, *settled = lax.optimization_barrier((own, *settled))
             sent = jnp.where(low == 0, mine_last, mine)
             own = own + shifted(sent, "l", 1)
             break
@@ -320,7 +315,6 @@
         mine_last = added(mine_last, shifted(other_last, "c", 1))
         moving_last = shifted(mine_last, "l", 1)
         mine, mine_last = lax.optimization_barrier((mine, mine_last))
-        mine, *settled = lax.optimization_barrier((mine, *settled))
         part = ((K // 2, OWN), f32)
         mine, upper, lower = call(add_parts_kernel, "add_parts", 4, [VMEM, VMEM], [chunk, part, part], [mine, moving])
         image, gram = call(
@@ -347,11 +341,16 @@
             [other_last, dense, image, gram, gram_mine],
             work,
         )
-        halves = mine, mine_last
+        halves += [mine, mine_last]
     gram = call(gram_kernel, "gram", 50, [VMEM], [((K // 2, 2 * K), f32)], [own])
     gram = summed_by_all(summed_by_all(gram + shifted(gram, "c", 1), PLANE), ("h", "l"))
     return call(
-        finish_kernel, "finish", 50, [VMEM] * (ITERS + 1), [((ITERS, K, OWN), f32)], [gram, own, *settled]
+        finish_kernel,
+        "finish",
+        50,
+        [SMEM] + [VMEM] * (3 * ITERS - 1),
+        [((ITERS, K, OWN), f32)],
+        [turn, gram, *halves, own, *inverses],
     )
 
 

time: 283 us -> 284 us (level)
  waiting for transfers between devices: 37.8 us -> 40.8 us
    ppermute x25, waiting for transfers between devices: 37.8 us -> 40.8 us  [shifted(): return lax.ppermute(x, axis, [(i, (i + by) % count) for i in range(count)])]
    pallas_call x45 -> x42, Pallas kernels: 43.1 us -> 40.9 us  [call(): pl.pallas_call(kernel, out_shape=shapes, in_specs=ins, out_specs=(VMEM,)...]
  transfers between devices with their start and end apart: 25 -> 25, of which waited for: 23 -> 23; matrix products, arithmetic and copies ran while one was open for 0% -> 0% of each run, Pallas kernels for 5% -> 4%
where the time goes in v6:
time: 284 us; the launch traced here: 280 us
  blocking collectives  173 us (61%)
  Pallas kernels  40.9 us (14%)
  waiting for transfers between devices  40.8 us (14%)
  starting transfers between devices  21.2 us (7%)
    all_to_all x4, blocking collectives, summed_over_blk(): shares = lax.all_to_all(packed, PLANE, 0, 0, tiled=True)  53 us
    all_to_all x4, blocking collectives, summed_over_blk(): shares = lax.all_to_all(shared(shares, 4), 'h', 0, 0, tiled=True)  48.7 us
    all_to_all x4, blocking collectives, summed_over_blk(): return lax.all_to_all(shared(shares, PEERS), PLANE, 0, 0, tiled=True)  47.8 us
    pallas_call x42, Pallas kernels, call(): pl.pallas_call(kernel, out_shape=shapes, in_specs=ins, out_specs=(VMEM,)...  40.9 us
    ppermute x25, waiting for transfers between devices, shifted(): return lax.ppermute(x, axis, [(i, (i + by) % count) for i in range(count)])  40.8 us
    all_to_all x2, blocking collectives, summed_by_all(): lax.all_to_all(jnp.broadcast_to(x[None], (count, *x.shape)), axes, 0, 0,...  23.4 us
    ppermute x25, starting transfers between devices, shifted(): return lax.ppermute(x, axis, [(i, (i + by) % count) for i in range(count)])  21.2 us
  transfers between devices with their start and end apart: 25, of which 23 were waited for; matrix products, arithmetic and copies ran while one was open for 0% of the time, Pallas kernels for 4%

profile of v6, /device:TPU:2, one launch (start us, length us, event | category | flops | bytes accessed | tf_op | source)
XLA Modules:
  0.0 279.6 jit_solution(16669998118159717420)
XLA Ops:
  3.1 9.7 %start.1 = (bf16[1024,4096]{1,0:T(8,128)(2,1)S(1)}, f32[16,40,128]{2,1,0:T(8,128)S(1)}) custom-call(s32[256]{0:T(256)S(1)} %bitcast.6, s32[256]{0:T(256)S(1)} %bitcast.7, s32[1]{0:T(128)} %bitcast.5.live, s32[2]{0:T(128)S(1)} %pad_add_fusion.turn, bf16[256,128,128]{2,1,0:T(8,128)(2,1)} %tiles.1, bf16[64,4096]{1,0:T(8,128)(2,1)S(1)} %copy-done), custom_call_target="tpu_custom_call" | custom-call | flops 536870912 | bytes 17631244 | tf_op jit(solution)/shard_map/start/pallas_call | solution.py:247
  12.9 15.3 %all_to_all.70.parts = f32[16,40,128]{2,1,0:T(8,128)S(1)} all-to-all(f32[16,40,128]{2,1,0:T(8,128)S(1)} %get-tuple-element.66), channel_id=1, replica_groups=mesh['y'=4,'x'=4,'h'=4,'l'=2,'c'=2] {'y','x'}, dimensions={0} | all-to-all | bytes 655360 | tf_op jit(solution)/shard_map/all_to_all | solution.py:269
  28.2 16.6 %all_to_all.71.parts = f32[4,40,128]{2,1,0:T(8,128)S(1)} all-to-all(f32[4,40,128]{2,1,0:T(8,128)S(1)} %share.8), channel_id=1, replica_groups=mesh['y'=4,'x'=4,'h'=4,'l'=2,'c'=2] {'h'}, dimensions={0} | all-to-all | bytes 163840 | tf_op jit(solution)/shard_map/all_to_all | solution.py:270
  44.8 11.9 %all_to_all.72.packed = f32[16,40,128]{2,1,0:T(8,128)S(1)} all-to-all(f32[16,40,128]{2,1,0:T(8,128)S(1)} %share.9), channel_id=1, replica_groups=mesh['y'=4,'x'=4,'h'=4,'l'=2,'c'=2] {'y','x'}, dimensions={0} | all-to-all | bytes 655360 | tf_op jit(solution)/shard_map/all_to_all | solution.py:271
  61.5 7.0 %collective-permute-done.2.b = f32[64,1024]{1,0:T(8,128)S(1)} collective-permute-done((f32[64,1024]{1,0:T(8,128)S(1)}, f32[64,1024]{1,0:T(8,128)S(1)}, u32[]{:S(2)}, u32[]{:S(2)}) %collective-permute-start.2) | collective-permute-done | bytes 262176 | tf_op jit(solution)/shard_map/ppermute | solution.py:236
  75.9 12.6 %all_to_all.73.parts = f32[16,40,128]{2,1,0:T(8,128)S(1)} all-to-all(f32[16,40,128]{2,1,0:T(8,128)S(1)} %forward_last.3), channel_id=1, replica_groups=mesh['y'=4,'x'=4,'h'=4,'l'=2,'c'=2] {'y','x'}, dimensions={0} | all-to-all | bytes 655360 | tf_op jit(solution)/shard_map/all_to_all | solution.py:269
  88.5 10.7 %all_to_all.74.parts = f32[4,40,128]{2,1,0:T(8,128)S(1)} all-to-all(f32[4,40,128]{2,1,0:T(8,128)S(1)} %share.10), channel_id=1, replica_groups=mesh['y'=4,'x'=4,'h'=4,'l'=2,'c'=2] {'h'}, dimensions={0} | all-to-all | bytes 163840 | tf_op jit(solution)/shard_map/all_to_all | solution.py:270
  99.3 12.1 %all_to_all.75.packed = f32[16,40,128]{2,1,0:T(8,128)S(1)} all-to-all(f32[16,40,128]{2,1,0:T(8,128)S(1)} %share.11), channel_id=1, replica_groups=mesh['y'=4,'x'=4,'h'=4,'l'=2,'c'=2] {'y','x'}, dimensions={0} | all-to-all | bytes 655360 | tf_op jit(solution)/shard_map/all_to_all | solution.py:271
  111.4 3.6 %backward.5 = (f32[64,1024]{1,0:T(8,128)S(1)}, f32[64,1024]{1,0:T(8,128)S(1)}, bf16[64,1024]{1,0:T(8,128)(2,1)S(1)}, f32[64,64]{1,0:T(8,128)S(1)}) custom-call(f32[16,40,128]{2,1,0:T(8,128)S(1)} %all_to_all.75.packed, bf16[1024,4096]{1,0:T(8,128)(2,1)S(1)} %get-tuple-element.67.dense), custom_call_target="tpu_custom_call" | custom-call | flops 268435456 | bytes 9388032 | tf_op jit(solution)/shard_map/backward/pallas_call | solution.py:247
  118.9 7.0 %collective-permute-done.9.b = f32[64,1024]{1,0:T(8,128)S(1)} collective-permute-done((f32[64,1024]{1,0:T(8,128)S(1)}, f32[64,1024]{1,0:T(8,128)S(1)}, u32[]{:S(2)}, u32[]{:S(2)}) %collective-permute-start.9) | collective-permute-done | bytes 262176 | tf_op jit(solution)/shard_map/ppermute | solution.py:236
  133.4 12.6 %all_to_all.76.parts = f32[16,40,128]{2,1,0:T(8,128)S(1)} all-to-all(f32[16,40,128]{2,1,0:T(8,128)S(1)} %forward_last.4), channel_id=1, replica_groups=mesh['y'=4,'x'=4,'h'=4,'l'=2,'c'=2] {'y','x'}, dimensions={0} | all-to-all | bytes 655360 | tf_op jit(solution)/shard_map/all_to_all | solution.py:269
  146.0 10.7 %all_to_all.77.parts = f32[4,40,128]{2,1,0:T(8,128)S(1)} all-to-all(f32[4,40,128]{2,1,0:T(8,128)S(1)} %share.12), channel_id=1, replica_groups=mesh['y'=4,'x'=4,'h'=4,'l'=2,'c'=2] {'h'}, dimensions={0} | all-to-all | bytes 163840 | tf_op jit(solution)/shard_map/all_to_all | solution.py:270
  156.7 11.9 %all_to_all.78.packed = f32[16,40,128]{2,1,0:T(8,128)S(1)} all-to-all(f32[16,40,128]{2,1,0:T(8,128)S(1)} %share.13), channel_id=1, replica_groups=mesh['y'=4,'x'=4,'h'=4,'l'=2,'c'=2] {'y','x'}, dimensions={0} | all-to-all | bytes 655360 | tf_op jit(solution)/shard_map/all_to_all | solution.py:271
  168.6 3.6 %backward.6 = (f32[64,1024]{1,0:T(8,128)S(1)}, f32[64,1024]{1,0:T(8,128)S(1)}, bf16[64,1024]{1,0:T(8,128)(2,1)S(1)}, f32[64,64]{1,0:T(8,128)S(1)}) custom-call(f32[16,40,128]{2,1,0:T(8,128)S(1)} %all_to_all.78.packed, bf16[1024,4096]{1,0:T(8,128)(2,1)S(1)} %get-tuple-element.67.dense), custom_call_target="tpu_custom_call" | custom-call | flops 268435456 | bytes 9388032 | tf_op jit(solution)/shard_map/backward/pallas_call | solution.py:247
  173.1 9.9 %collective-permute-start.15 = (f32[64,1024]{1,0:T(8,128)S(1)}, f32[64,1024]{1,0:T(8,128)S(1)}, u32[]{:S(2)}, u32[]{:S(2)}) collective-permute-start(f32[64,1024]{1,0:T(8,128)S(1)} %get-tuple-element.106), channel_id=1, source_target_pairs={{0,1},{1,0},{2,3},{3,2},{4,5},{5,4},{6,7},{7,6},{8,9},{9,8},{10,11... | collective-permute-start | bytes 786440 | tf_op jit(solution)/shard_map/ppermute | solution.py:236
  185.3 7.0 %collective-permute-done.16.b = f32[64,1024]{1,0:T(8,128)S(1)} collective-permute-done((f32[64,1024]{1,0:T(8,128)S(1)}, f32[64,1024]{1,0:T(8,128)S(1)}, u32[]{:S(2)}, u32[]{:S(2)}) %collective-permute-start.16) | collective-permute-done | bytes 262176 | tf_op jit(solution)/shard_map/ppermute | solution.py:236
  199.6 12.6 %all_to_all.79.parts = f32[16,40,128]{2,1,0:T(8,128)S(1)} all-to-all(f32[16,40,128]{2,1,0:T(8,128)S(1)} %forward_last.5), channel_id=1, replica_groups=mesh['y'=4,'x'=4,'h'=4,'l'=2,'c'=2] {'y','x'}, dimensions={0} | all-to-all | bytes 655360 | tf_op jit(solution)/shard_map/all_to_all | solution.py:269
  212.2 10.7 %all_to_all.80.parts = f32[4,40,128]{2,1,0:T(8,128)S(1)} all-to-all(f32[4,40,128]{2,1,0:T(8,128)S(1)} %share.14), channel_id=1, replica_groups=mesh['y'=4,'x'=4,'h'=4,'l'=2,'c'=2] {'h'}, dimensions={0} | all-to-all | bytes 163840 | tf_op jit(solution)/shard_map/all_to_all | solution.py:270
  223.0 11.9 %all_to_all.81.packed = f32[16,40,128]{2,1,0:T(8,128)S(1)} all-to-all(f32[16,40,128]{2,1,0:T(8,128)S(1)} %share.15), channel_id=1, replica_groups=mesh['y'=4,'x'=4,'h'=4,'l'=2,'c'=2] {'y','x'}, dimensions={0} | all-to-all | bytes 655360 | tf_op jit(solution)/shard_map/all_to_all | solution.py:271
  234.9 3.6 %backward.7 = (f32[64,1024]{1,0:T(8,128)S(1)}, f32[64,1024]{1,0:T(8,128)S(1)}, bf16[64,1024]{1,0:T(8,128)(2,1)S(1)}, f32[64,64]{1,0:T(8,128)S(1)}) custom-call(f32[16,40,128]{2,1,0:T(8,128)S(1)} %all_to_all.81.packed, bf16[1024,4096]{1,0:T(8,128)(2,1)S(1)} %get-tuple-element.67.dense), custom_call_target="tpu_custom_call" | custom-call | flops 268435456 | bytes 9388032 | tf_op jit(solution)/shard_map/backward/pallas_call | solution.py:247
  242.0 7.9 %collective-permute-done.23 = f32[64,1024]{1,0:T(8,128)S(1)} collective-permute-done((f32[64,1024]{1,0:T(8,128)S(1)}, f32[64,1024]{1,0:T(8,128)S(1)}, u32[]{:S(2)}, u32[]{:S(2)}) %collective-permute-start.23) | collective-permute-done | bytes 262176 | tf_op jit(solution)/shard_map/ppermute | solution.py:236
  251.5 11.9 %all_to_all.82 = f32[16,32,128]{2,1,0:T(8,128)S(1)} all-to-all(f32[16,32,128]{2,1,0:T(8,128)S(1)} %broadcast_in_dim.4), channel_id=1, replica_groups=mesh['y'=4,'x'=4,'h'=4,'l'=2,'c'=2] {'y','x'}, dimensions={0} | all-to-all | bytes 524288 | tf_op jit(solution)/shard_map/all_to_all | solution.py:241
  263.5 11.5 %all_to_all.83 = f32[8,32,128]{2,1,0:T(8,128)S(1)} all-to-all(f32[8,32,128]{2,1,0:T(8,128)S(1)} %broadcast_in_dim.5), channel_id=1, replica_groups=mesh['y'=4,'x'=4,'h'=4,'l'=2,'c'=2] {'h','l'}, dimensions={0} | all-to-all | bytes 262144 | tf_op jit(solution)/shard_map/all_to_all | solution.py:241
  275.0 4.4 %finish.1 = f32[4,64,1024]{2,1,0:T(8,128)} custom-call(s32[2]{0:T(128)S(1)} %pad_add_fusion.turn, f32[32,128]{1,0:T(8,128)S(1)} %reduce_sum.19.gram, f32[64,1024]{1,0:T(8,128)S(1)} %get-tuple-element.75.mine.refs_0_, f32[64,1024]{1,0:T(8,128)S(1)} %add.24.mine.refs_1_, f32[64,1024]{1,0:T(8,128)S(1)} %get-tuple-element.92.mine.refs_2_, ...), custom_call_target="tpu_custom_call" | custom-call | bytes 2949128 | tf_op jit(solution)/shard_map/finish/pallas_call | solution.py:247
  (96 shorter events, 41.9 us)
Async XLA Ops:
  57.6 1.6 collective-permute-start
  58.5 1.8 collective-permute-start.1
  59.2 9.2 %collective-permute-start.2 = (f32[64,1024]{1,0:T(8,128)S(1)}, f32[64,1024]{1,0:T(8,128)S(1)}, u32[]{:S(2)}, u32[]{:S(2)}) collective-permute-start(f32[64,1024]{1,0:T(8,128)S(1)} %add.22.a), channel_id=1, source_target_pairs={{0,2},{2,0},{1,3},{3,1},{4,6},{6,4},{5,7},{7,5},{8,10},{10,8},{9,1... | collective-permute-start | bytes 786440 | tf_op jit(solution)/shard_map/ppermute | solution.py:236
  60.3 12.9 %collective-permute-start.5 = (f32[64,1024]{1,0:T(8,128)S(1)}, f32[64,1024]{1,0:T(8,128)S(1)}, u32[]{:S(2)}, u32[]{:S(2)}) collective-permute-start(f32[64,1024]{1,0:T(8,128)S(1)} %add.23.a), channel_id=1, source_target_pairs={{0,2},{2,0},{1,3},{3,1},{4,6},{6,4},{5,7},{7,5},{8,10},{10,8},{9,1... | collective-permute-start | bytes 786440 | tf_op jit(solution)/shard_map/ppermute | solution.py:236
  68.5 1.4 collective-permute-start.3
  68.6 1.5 collective-permute-start.4
  73.3 1.6 collective-permute-start.6
  115.0 1.6 collective-permute-start.7
  115.9 1.7 collective-permute-start.8
  116.6 9.2 %collective-permute-start.9 = (f32[64,1024]{1,0:T(8,128)S(1)}, f32[64,1024]{1,0:T(8,128)S(1)}, u32[]{:S(2)}, u32[]{:S(2)}) collective-permute-start(f32[64,1024]{1,0:T(8,128)S(1)} %add.25.a), channel_id=1, source_target_pairs={{0,2},{2,0},{1,3},{3,1},{4,6},{6,4},{5,7},{7,5},{8,10},{10,8},{9,1... | collective-permute-start | bytes 786440 | tf_op jit(solution)/shard_map/ppermute | solution.py:236
  117.7 13.0 %collective-permute-start.12 = (f32[64,1024]{1,0:T(8,128)S(1)}, f32[64,1024]{1,0:T(8,128)S(1)}, u32[]{:S(2)}, u32[]{:S(2)}) collective-permute-start(f32[64,1024]{1,0:T(8,128)S(1)} %add.26.a), channel_id=1, source_target_pairs={{0,2},{2,0},{1,3},{3,1},{4,6},{6,4},{5,7},{7,5},{8,10},{10,8},{9,1... | collective-permute-start | bytes 786440 | tf_op jit(solution)/shard_map/ppermute | solution.py:236
  125.9 1.4 collective-permute-start.10
  126.0 1.5 collective-permute-start.11
  130.7 1.6 collective-permute-start.13
  172.2 10.8 %collective-permute-start.14 = (f32[64,1024]{1,0:T(8,128)S(1)}, f32[64,1024]{1,0:T(8,128)S(1)}, u32[]{:S(2)}, u32[]{:S(2)}) collective-permute-start(f32[64,1024]{1,0:T(8,128)S(1)} %get-tuple-element.103), channel_id=1, source_target_pairs={{0,1},{1,0},{2,3},{3,2},{4,5},{5,4},{6,7},{7,6},{8,9},{9,8},{10,11... | collective-permute-start | bytes 786440 | tf_op jit(solution)/shard_map/ppermute | solution.py:236
  173.1 11.0 %collective-permute-start.15 = (f32[64,1024]{1,0:T(8,128)S(1)}, f32[64,1024]{1,0:T(8,128)S(1)}, u32[]{:S(2)}, u32[]{:S(2)}) collective-permute-start(f32[64,1024]{1,0:T(8,128)S(1)} %get-tuple-element.106), channel_id=1, source_target_pairs={{0,1},{1,0},{2,3},{3,2},{4,5},{5,4},{6,7},{7,6},{8,9},{9,8},{10,11... | collective-permute-start | bytes 786440 | tf_op jit(solution)/shard_map/ppermute | solution.py:236
  183.0 9.3 %collective-permute-start.16 = (f32[64,1024]{1,0:T(8,128)S(1)}, f32[64,1024]{1,0:T(8,128)S(1)}, u32[]{:S(2)}, u32[]{:S(2)}) collective-permute-start(f32[64,1024]{1,0:T(8,128)S(1)} %add.28.a), channel_id=1, source_target_pairs={{0,2},{2,0},{1,3},{3,1},{4,6},{6,4},{5,7},{7,5},{8,10},{10,8},{9,1... | collective-permute-start | bytes 786440 | tf_op jit(solution)/shard_map/ppermute | solution.py:236
  184.2 12.8 %collective-permute-start.19 = (f32[64,1024]{1,0:T(8,128)S(1)}, f32[64,1024]{1,0:T(8,128)S(1)}, u32[]{:S(2)}, u32[]{:S(2)}) collective-permute-start(f32[64,1024]{1,0:T(8,128)S(1)} %add.29.a), channel_id=1, source_target_pairs={{0,2},{2,0},{1,3},{3,1},{4,6},{6,4},{5,7},{7,5},{8,10},{10,8},{9,1... | collective-permute-start | bytes 786440 | tf_op jit(solution)/shard_map/ppermute | solution.py:236
  192.3 1.4 collective-permute-start.17
  192.4 1.5 collective-permute-start.18
  197.0 1.6 collective-permute-start.20
  238.4 1.6 collective-permute-start.21
  239.4 1.7 collective-permute-start.22
  241.2 8.7 %collective-permute-start.23 = (f32[64,1024]{1,0:T(8,128)S(1)}, f32[64,1024]{1,0:T(8,128)S(1)}, u32[]{:S(2)}, u32[]{:S(2)}) collective-permute-start(f32[64,1024]{1,0:T(8,128)S(1)} %broadcast_select_fusion), channel_id=1, source_target_pairs={{0,2},{2,0},{1,3},{3,1},{4,6},{6,4},{5,7},{7,5},{8,10},{10,8},{9,1... | collective-permute-start | bytes 786440 | tf_op jit(solution)/shard_map/ppermute | solution.py:236
  (4 other events, 3.6 us)
